TPU v7x, 128 devices: a whole 4x4x4 slice. The times are simulated.
128 devices in a mesh: prow: 8 (over z, x_lo), pcol: 16 (over x_hi, y, core).
Axes of the slice: x: 4 (x_hi: 2, x_lo: 2; x = x_hi * 2 + x_lo), y: 4, z: 4, core: 2. Of those that a mesh axis runs over, the one named last changes fastest.
Arguments:
- leaf_rhs: float32 [8, 32, 256, 256], P('prow', 'pcol'), may hold values from -6 to 6
- leaf_inverse: float32 [8, 32, 256, 256], P('prow', 'pcol'), as said below
- off_blocks: float32 [8, 2, 8, 32, 512, 256], P('prow', None, None, 'pcol'), may hold values from -0.09375 to 0.09375
- ancestor_rows: int32 [8, 2, 8, 32], P('prow', None, None, 'pcol'), may hold values from 0 to 31
- block_present: int32 [8, 2, 8, 32], P('prow', None, None, 'pcol'), may hold values 0 or 1
- top_rhs: float32 [256, 512, 256], P(('prow', 'pcol')), may hold values from -6 to 6
- top_inverse: float32 [256, 512, 512], P(('prow', 'pcol')), as said below
Outputs:
- leaf_solution: float32 [8, 32, 256, 256], P('prow', 'pcol')
- top_solution: float32 [256, 512, 256], P(('prow', 'pcol'))
Inputs may be any that keep to these rules, and one draw needn't show every extreme that they name: `leaf_inverse`: each block is lower triangular with diagonal entries between 1 and 2. `top_inverse`: each block is lower triangular with diagonal entries between 1 and 2.
All inputs are finite; a program needn't handle non-finite values. No bound on the sum of `block_present` on one device may be relied on, other than what follows from the above.
Results may differ from a plain program's by a relative error of at most 0.0001.
Values sent between devices are 32-bit elements; how exact they have to be, the bound alone decides.
A program may use at most 128 MiB of HBM per device.

v0:
```python
import jax
import jax.numpy as jnp
from jax import lax
from jax.sharding import PartitionSpec as P


def block_terms(blocks, pieces):
    return jnp.einsum("auvij,uvjr->auvir", blocks, pieces, precision=lax.Precision.HIGHEST)


def selector(rows_index, present, count):
    flat_rows = rows_index.reshape(-1)
    flat_keep = present.reshape(-1).astype(jnp.float32)
    wanted = lax.broadcasted_iota(jnp.int32, (count, flat_rows.shape[0]), 0)
    return jnp.where(
        wanted == flat_rows[None, :], flat_keep[None, :], jnp.zeros_like(flat_keep)[None, :]
    )


def spread_rows(terms, choose):
    width = terms.shape[-2] * terms.shape[-1]
    flat = terms.reshape(-1, width)
    result = jnp.dot(
        choose, flat, precision=lax.Precision.HIGHEST, preferred_element_type=jnp.float32
    )
    return result.reshape(choose.shape[0], terms.shape[-2], terms.shape[-1])


def gather_pieces(solved):
    return lax.all_gather(solved, "prow", axis=0, tiled=True)


def solve_columns(leaf_rhs, leaf_inverse, blocks, rows_index, present, top_rhs, top_inverse):
    solved = jnp.einsum("uvij,uvjr->uvir", leaf_inverse, leaf_rhs, precision=lax.Precision.HIGHEST)
    own_rows = top_rhs.shape[0]
    group_rows = own_rows * lax.axis_size("pcol")
    pieces = gather_pieces(solved)
    partial_update = spread_rows(
        block_terms(blocks, pieces), selector(rows_index, present, group_rows)
    )
    update = lax.psum_scatter(partial_update, "pcol", scatter_dimension=0, tiled=True)
    top = jnp.einsum("kij,kjr->kir", top_inverse, top_rhs - update, precision=lax.Precision.HIGHEST)
    return (solved, top)


def per_device(
    leaf_rhs, leaf_inverse, off_blocks, ancestor_rows, block_present, top_rhs, top_inverse
):
    blocks = off_blocks[0]
    rows_index = ancestor_rows[0]
    present = block_present[0]
    return solve_columns(leaf_rhs, leaf_inverse, blocks, rows_index, present, top_rhs, top_inverse)


def solution(mesh):
    return jax.shard_map(
        per_device,
        mesh=mesh,
        in_specs=(
            P("prow", "pcol", None, None),
            P("prow", "pcol", None, None),
            P("prow", None, None, "pcol", None, None),
            P("prow", None, None, "pcol"),
            P("prow", None, None, "pcol"),
            P(("prow", "pcol"), None, None),
            P(("prow", "pcol"), None, None),
        ),
        out_specs=(P("prow", "pcol", None, None), P(("prow", "pcol"), None, None)),
        check_vma=False,
    )
```

profile of v0, /device:TPU:1, one launch (start us, length us, event | category | flops | bytes accessed | tf_op | source)
XLA Modules:
  0.0 365.2 jit_solution(5790573304907066190)
XLA Ops:
  7.2 0.0 copy-start
  7.2 0.0 all-gather.3.cloned.1.call-start
  7.2 2.8 fusion.9
  10.0 0.0 all-gather.3.cloned.1.call-update
  10.0 0.0 reduce-scatter.2.cloned.1.call-start
  10.1 0.7 convert_element_type.10
  10.8 0.1 copy.32
  10.9 0.1 convert_element_type.11
  10.9 0.8 copy.31
  11.7 0.1 eq.10
  11.8 92.4 %all-gather.3.cloned.1.call-done = f32[16,256,256]{2,1,0:T(8,128)} async-done(((f32[2,256,256]{2,1,0:T(8,128)}), f32[16,256,256]{2,1,0:T(8,128)}) %all-gather.3.cloned.1.call-update) | async-done | bytes 4194320 | tf_op jit(solution)/shard_map/all_gather | solution.py:30
  104.2 34.5 %fusion.5 = f32[2,8,2,512,256]{3,4,0,2,1:T(8,128)} fusion(f32[8,2,256,256,1]{3,2,4,1,0:T(8,128)} %bitcast.43, f32[1,2,8,2,512,256]{5,4,3,2,1,0:T(8,128)} %param.9), kind=kOutput, calls=%fused_computation.5 | convolution fusion | flops 12884901888 | bytes 37748736 | tf_op jit(solution)/shard_map/auvij,uvjr->auvir/dot_general | solution.py:8
  138.7 17.4 %copy.35 = f32[2,8,2,512,256]{4,3,2,1,0:T(8,128)} copy(f32[2,8,2,512,256]{3,4,0,2,1:T(8,128)} %fusion.5) | data formatting | bytes 33554432 | tf_op jit(solution)/shard_map/auvij,uvjr->auvir/transpose | solution.py:8
  156.1 32.6 %fusion = f32[32,512,256]{2,0,1:T(8,128)} fusion(f32[32]{0:T(128)S(1)} %convert_element_type.11, s32[32]{0:T(128)S(1)} %eq.10, f32[4,8,512,256]{3,2,1,0:T(8,128)} %bitcast.42), kind=kOutput, calls=%fused_computation | convolution fusion | flops 1610614784 | bytes 33554688 | tf_op jit(solution)/shard_map/dot_general | solution.py:23
  188.7 15.8 %copy.37 = f32[32,512,256]{2,1,0:T(8,128)} copy(f32[32,512,256]{2,0,1:T(8,128)} %fusion) | data formatting | bytes 33554432 | tf_op jit(solution)/shard_map/dot_general | solution.py:23
  204.5 0.0 reduce-scatter.2.cloned.1.call-update
  204.5 147.4 %reduce-scatter.2.cloned.1.call-done = f32[2,512,256]{2,1,0:T(8,128)} async-done(((f32[32,512,256]{2,1,0:T(8,128)}), f32[2,512,256]{2,1,0:T(8,128)}) %reduce-scatter.2.cloned.1.call-update) | async-done | bytes 1048592 | tf_op jit(solution)/shard_map/reduce_scatter | solution.py:41
  351.9 0.0 copy-done
  351.9 5.1 %convolution_bitcast_fusion = f32[2,512,256]{1,2,0:T(8,128)S(1)} fusion(f32[2,512,512]{2,1,0:T(8,128)S(1)} %copy-done, f32[2,512,256]{2,1,0:T(8,128)} %param.12, f32[2,512,256]{2,1,0:T(8,128)} %reduce-scatter.2.cloned.1.call-done), kind=kOutput, calls=%fused_computation.6 | convolution fusion | flops 1610874880 | bytes 5242880 | tf_op jit(solution)/shard_map/kij,kjr->kir/dot_general | solution.py:42
  357.0 1.3 copy.39
Async XLA Ops:
  7.2 344.8 %copy-start = (f32[2,512,512]{2,1,0:T(8,128)S(1)}, f32[2,512,512]{2,1,0:T(8,128)}, u32[]{:S(2)}) copy-start(f32[2,512,512]{2,1,0:T(8,128)} %param.13) | copy-start | bytes 6291460
  7.2 97.0 %all-gather.3.cloned.1.call-start = ((), (), s32[]{:S(2)}) async-start(), calls=%async_computation.2 | async-start | bytes 4718592 | tf_op jit(solution)/shard_map/all_gather | solution.py:30
  10.0 341.9 %reduce-scatter.2.cloned.1.call-start = ((), (), s32[]{:S(2)}) async-start(), calls=%async_computation.1 | async-start | bytes 17825792 | tf_op jit(solution)/shard_map/reduce_scatter | solution.py:41
Sparse Core Ops, SparseCore 0:
  10.2 93.9 all-gather.2
  204.7 147.2 reduce-scatter.1
where the time goes:
time: 366 us; the launch traced here: 365 us
  waiting for transfers between devices  240 us (66%)
  matrix products  75 us (20%)
  local copies, waits for them, and re-layouts  35.5 us (10%)
  between operations  14.1 us (4%)
    reduce_scatter x1, waiting for transfers between devices, solve_columns(): lax.psum_scatter(partial_update, 'pcol', scatter_dimension=0, tiled=True)  147 us
    all_gather x1, waiting for transfers between devices, gather_pieces(): return lax.all_gather(solved, 'prow', axis=0, tiled=True)  92.4 us
    dot_general x1, matrix products, block_terms(): jnp.einsum('auvij,uvjr->auvir', blocks, pieces, precision=lax.Precision.H...  34.5 us
    dot_general x1, matrix products, spread_rows(): jnp.dot(choose, flat, precision=lax.Precision.HIGHEST, preferred_element_...  32.6 us
    transpose x1, local copies, waits for them, and re-layouts, block_terms(): jnp.einsum('auvij,uvjr->auvir', blocks, pieces, precision=lax.Precision.H...  17.4 us
    dot_general x1, local copies, waits for them, and re-layouts, spread_rows(): jnp.dot(choose, flat, precision=lax.Precision.HIGHEST, preferred_element_...  15.8 us
  transfers between devices with their start and end apart: 2, of which 2 were waited for; matrix products, arithmetic and copies ran while one was open for 0% of the time, Pallas kernels for 0%

commit v1 on v0

v1 whole, which is shorter than its diff:
```python
import jax
import jax.numpy as jnp
from jax import lax
from jax.experimental import pallas as pl
from jax.experimental.pallas import tpu as pltpu
from jax.sharding import PartitionSpec as P

MESH = pl.DeviceIdType.MESH
F32, BF16 = jnp.float32, jnp.bfloat16
W1, W2, HALF = 256, 512, 128
STEPS = 8
BUFS = 3
CUT = 288
NONE = 32

UNITS = (
    (1, 2, 0), (1, 2, 1), (0, 2, 0), (0, 2, 1),
    (1, 1, 1), (1, 3, 0), (0, 1, 1), (0, 3, 0),
    (1, 1, 0), (1, 3, 1), (0, 1, 0), (0, 3, 1),
    (1, 0, 0), (1, 0, 1), (0, 0, 0), (0, 0, 1),
)
Y_SEND = ((0, 2, 4, 6, 8, 10), (1, 3, 5, 7, 9, 11))
Y_ADD = ((8, 10, 13, 15, 12, 14), (9, 11, 12, 14, 13, 15))
X_SEND = (0, 1, 4, 5, 8, 9, 12, 13)
XY_SEND = ((2, 6, 10), (3, 7, 11))
XY_ADD = ((10, 15, 14), (11, 14, 15))


def split(value):
    high = value.astype(BF16)
    return high, (value - high.astype(F32)).astype(BF16)


def dot(a, b):
    return jnp.dot(a, b, preferred_element_type=F32)


def times(a_high, a_low, both, high):
    wide = dot(a_high, both)
    return wide[:, :HALF] + wide[:, HALF:] + dot(a_low, high)


def kernel(
    meta, leaf_rhs, leaf_inv, off_blocks, top_rhs, top_inv, leaf_out, top_out,
    x, w, blocks, chain, give, s, yr, xyr, xr, x2r, rhs, inv, inv_high, inv_low,
    block_sem, top_sem, az_s, az_r, ax_s, ax_r, core_s, core_r, y_s, y_r, xy_s, xy_r, x_s, x_r, x2_s, x2_r,
):
    row, col = lax.axis_index("prow"), lax.axis_index("pcol")
    z, xl = row // 2, row % 2
    xh, y, core = col // 8, (col // 2) % 4, col % 2

    def rows_at(dz, dx):
        return ((z + dz) % 4) * 2 + (xl + dx) % 2

    def at(dxh, dy, dcore):
        return ((xh + dxh) % 2) * 8 + ((y + dy) % 4) * 2 + (core + dcore) % 2

    x_near = (rows_at(0, 1), col)
    z_to = ((rows_at(1, 0), col), (rows_at(3, 0), col))
    other_core = (row, at(0, 0, 1))
    x_far = (row, at(1, 0, 0))
    y_to = ((row, at(0, 1, 0)), (row, at(0, 3, 0)))
    order = [rows_at(*d) for d in ((0, 0), (0, 1), (3, 0), (1, 0), (2, 0), (3, 1), (1, 1), (2, 1))]

    def send(src, dst, send_sem, recv_sem, device):
        return pltpu.make_async_remote_copy(
            src_ref=src, dst_ref=dst, send_sem=send_sem, recv_sem=recv_sem, device_id=device, device_id_type=MESH
        )

    def fetch(g):
        u = order[g % STEPS]
        return pltpu.make_async_copy(off_blocks.at[0, :, u], blocks.at[g % BUFS], block_sem.at[g % BUFS])

    for g in range(BUFS):
        fetch(g).start()
    fetch_rhs = pltpu.make_async_copy(top_rhs, rhs, top_sem.at[0])
    fetch_inv = pltpu.make_async_copy(top_inv, inv, top_sem.at[1])
    fetch_rhs.start()
    fetch_inv.start()

    barrier = pltpu.get_barrier_semaphore()
    partners = (x_near, *z_to, other_core, x_far, *y_to)
    for partner in partners:
        pl.semaphore_signal(barrier, inc=1, device_id=partner, device_id_type=MESH)

    chain[NONE] = jnp.zeros((W2, HALF), F32)

    def leaf(ch):
        for v in range(2):
            i_high, i_low = split(leaf_inv[0, v])
            r_high, r_low = split(leaf_rhs[0, v, :, ch * HALF : (ch + 1) * HALF])
            solved = times(i_high, i_low, jnp.concatenate([r_high, r_low], axis=1), r_high)
            x[ch, row, v] = solved
            leaf_out[0, v, :, ch * HALF : (ch + 1) * HALF] = solved

    def x_msg(ch, j, v):
        u = order[0] if j == 0 else order[4]
        ref = x.at[ch, u, v]
        return send(ref, ref, ax_s.at[ch, j, v], ax_r.at[ch, j, v], x_near)

    def z_msg(ch, d, j):
        u = (order[0], order[0], order[2 + d], order[1], order[1])[j]
        v = (d, 1 - d, d, 0, 1)[j]
        ref = x.at[ch, u, v]
        return send(ref, ref, az_s.at[ch, d, j], az_r.at[ch, d, j], z_to[d])

    def gather_own(ch):
        for j in range(2):
            x_msg(ch, 0, j).start()
            for d in range(2):
                z_msg(ch, d, j).start()

    def gather_near(ch):
        for d in range(2):
            z_msg(ch, d, 0).wait_recv()
            z_msg(ch, d, 2).start()
        for j in range(2):
            x_msg(ch, 0, j).wait_recv()
            for d in range(2):
                z_msg(ch, d, 3 + j).start()

    def gather_far(ch):
        for d in range(2):
            z_msg(ch, d, 2).wait_recv()
        for v in range(2):
            x_msg(ch, 1, v).start()

    def gather_wait(ch, step):
        if step in (2, 3):
            z_msg(ch, step - 2, 1).wait_recv()
        if step in (5, 6):
            for j in (3, 4):
                z_msg(ch, step - 5, j).wait_recv()
        if step == 7:
            for v in range(2):
                x_msg(ch, 1, v).wait_recv()

    def gather_sent(ch):
        for d in range(2):
            for j in range(5):
                z_msg(ch, d, j).wait_send()
        for j in range(2):
            for v in range(2):
                x_msg(ch, j, v).wait_send()

    def products(ch, step):
        g = ch * STEPS + step
        u = order[step]
        fetch(g).wait()
        for v in range(2):
            high, low = split(x[ch, u, v])
            w[v, :, :HALF] = high
            w[v, :, HALF:] = low

        def one(i, carry):
            v, a, tile = i // 4, (i // 2) % 2, i % 2
            tall = pl.ds(pl.multiple_of(tile * 256, 256), 256)
            before = meta[a * 16 + u * 2 + v]
            b_high, b_low = split(blocks[g % BUFS, a, v, tall, :])
            term = times(b_high, b_low, w[v], w[v, :, :HALF])
            chain[step * 4 + v * 2 + a, tall, :] = term + chain[before, tall, :]
            return carry

        lax.fori_loop(0, 8, one, 0)
        if g + BUFS < 2 * STEPS:
            fetch(g + BUFS).start()

    def number(i, its_core):
        dxh, dy, e = UNITS[i]
        return ((xh + dxh) % 2) * 16 + ((y + dy) % 4) * 4 + its_core * 2 + e

    def core_msg(ch, i):
        return send(give.at[i], s.at[ch, i], core_s.at[i], core_r.at[ch, i], other_core)

    def y_msg(ch, d, j):
        return send(
            s.at[ch, Y_SEND[d][j], pl.ds(0, CUT)], yr.at[ch, d, j], y_s.at[ch, d, j], y_r.at[ch, d, j], y_to[d]
        )

    def xy_msg(ch, d, j):
        return send(
            s.at[ch, XY_SEND[d][j], pl.ds(CUT, W2 - CUT)],
            xyr.at[ch, d, j],
            xy_s.at[ch, d, j],
            xy_r.at[ch, d, j],
            y_to[d],
        )

    def x_far_msg(ch, m):
        return send(
            s.at[ch, X_SEND[m], pl.ds(CUT, W2 - CUT)], xr.at[ch, m], x_s.at[ch, m], x_r.at[ch, m], x_far
        )

    def x_last_msg(ch, e):
        return send(s.at[ch, 12 + e, pl.ds(0, CUT)], x2r.at[ch, e], x2_s.at[ch, e], x2_r.at[ch, e], x_far)

    def share_core(ch):
        for i in range(16):
            if ch:
                core_msg(ch - 1, i).wait_send()
            give[i] = chain[meta[32 + number(i, 1 - core)]]
            core_msg(ch, i).start()

    def sum_core(ch):
        for i in range(16):
            core_msg(ch, i).wait_recv()
            s[ch, i] = s[ch, i] + chain[meta[32 + number(i, core)]]
            for d in range(2):
                if i in Y_SEND[d][:4]:
                    y_msg(ch, d, Y_SEND[d].index(i)).start()
            if i in X_SEND:
                x_far_msg(ch, X_SEND.index(i)).start()

    def y_add(ch, d, j):
        y_msg(ch, d, j).wait_recv()
        i = Y_ADD[d][j]
        s[ch, i, :CUT] = s[ch, i, :CUT] + yr[ch, d, j]

    def xy_add(ch, d, j):
        xy_msg(ch, d, j).wait_recv()
        i = XY_ADD[d][j]
        s[ch, i, CUT:] = s[ch, i, CUT:] + xyr[ch, d, j]

    def y_pass(ch, j):
        for d in range(2):
            y_add(ch, d, j)
            y_msg(ch, d, 4 + j).start()

    def x_add(ch, m):
        x_far_msg(ch, m).wait_recv()
        i = X_SEND[m] + 2
        s[ch, i, CUT:] = s[ch, i, CUT:] + xr[ch, m]
        for d in range(2):
            if i in XY_SEND[d][:2]:
                xy_msg(ch, d, XY_SEND[d].index(i)).start()

    def xy_pass(ch):
        for d in range(2):
            xy_add(ch, d, 0)
            xy_msg(ch, d, 2).start()

    def y_last(ch):
        for d, j in ((0, 2), (1, 2), (0, 4), (1, 4)):
            y_add(ch, d, j)
        for e in range(2):
            x_last_msg(ch, e).start()

    def finish(ch):
        for d, j in ((0, 3), (1, 3), (0, 5), (1, 5)):
            y_add(ch, d, j)
        for d, j in ((0, 1), (1, 1), (0, 2), (1, 2)):
            xy_add(ch, d, j)
        for e in range(2):
            x_last_msg(ch, e).wait_recv()
            i = 14 + e
            s[ch, i, :CUT] = s[ch, i, :CUT] + x2r[ch, e]
            cols = slice(ch * HALF, (ch + 1) * HALF)
            high, low = split(rhs[e, :, cols] - s[ch, i])
            both = jnp.concatenate([high, low], axis=1)
            top_out[e, :256, cols] = times(
                inv_high[e, :256, :256], inv_low[e, :256, :256], both[:256], high[:256]
            )
            top_out[e, 256:, cols] = times(inv_high[e, 256:], inv_low[e, 256:], both, high)

    leaf(0)
    pl.semaphore_wait(barrier, len(partners))
    gather_own(0)
    leaf(1)
    products(0, 0)
    gather_near(0)
    for step in range(1, 4):
        gather_wait(0, step)
        products(0, step)
    gather_far(0)
    for step in range(4, 8):
        gather_wait(0, step)
        products(0, step)
    gather_own(1)
    share_core(0)
    sum_core(0)
    gather_near(1)

    fetch_rhs.wait()
    fetch_inv.wait()

    def split_inv(i, carry):
        e, tall = i // 4, pl.ds(pl.multiple_of((i % 4) * 128, 128), 128)
        high, low = split(inv[e, tall, :])
        inv_high[e, tall, :] = high
        inv_low[e, tall, :] = low
        return carry

    lax.fori_loop(0, 8, split_inv, 0)

    for step in range(0, 2):
        products(1, step)
    y_pass(0, 0)
    for step in range(2, 4):
        gather_wait(1, step)
        products(1, step)
    gather_far(1)
    y_pass(0, 1)
    for step in range(4, 8):
        gather_wait(1, step)
        products(1, step)
    share_core(1)
    sum_core(1)
    for m in range(8):
        x_add(0, m)
    xy_pass(0)
    y_last(0)
    y_pass(1, 0)
    y_pass(1, 1)
    finish(0)
    for m in range(8):
        x_add(1, m)
    xy_pass(1)
    y_last(1)
    finish(1)

    for ch in range(2):
        gather_sent(ch)
        for d in range(2):
            for j in range(6):
                y_msg(ch, d, j).wait_send()
            for j in range(3):
                xy_msg(ch, d, j).wait_send()
        for m in range(8):
            x_far_msg(ch, m).wait_send()
        for e in range(2):
            x_last_msg(ch, e).wait_send()
    for i in range(16):
        core_msg(1, i).wait_send()


def chains(rows_index, present, row):
    u = lax.broadcasted_iota(jnp.int32, (2, 8, 2), 1)
    a = lax.broadcasted_iota(jnp.int32, (2, 8, 2), 0)
    v = lax.broadcasted_iota(jnp.int32, (2, 8, 2), 2)
    far = (u // 2 - row // 2 + 4) % 4
    near = (u + row) % 2
    step = jnp.where(
        far == 0, near, jnp.where(far == 3, 2 + 3 * near, jnp.where(far == 1, 3 + 3 * near, 4 + 3 * near))
    )
    rank = (step * 4 + v * 2 + a).reshape(-1)
    wanted = jnp.where(present != 0, rows_index, -1).reshape(-1)
    ask = jnp.concatenate([wanted, jnp.arange(32, dtype=jnp.int32)])
    limit = jnp.concatenate([rank, jnp.full((32,), 32, jnp.int32)])
    fits = (wanted[None, :] == ask[:, None]) & (rank[None, :] < limit[:, None])
    found = jnp.max(jnp.where(fits, rank[None, :], -1), axis=1)
    return jnp.where(found < 0, NONE, found)


def per_device(leaf_rhs, leaf_inverse, off_blocks, ancestor_rows, block_present, top_rhs, top_inverse):
    meta = chains(ancestor_rows[0], block_present[0], lax.axis_index("prow"))
    vmem = pl.BlockSpec(memory_space=pltpu.VMEM)
    smem = pl.BlockSpec(memory_space=pltpu.SMEM)
    anywhere = pl.BlockSpec(memory_space=pl.ANY)
    rest = W2 - CUT
    dma = pltpu.SemaphoreType.DMA
    return pl.pallas_call(
        kernel,
        out_shape=(
            jax.ShapeDtypeStruct(leaf_rhs.shape, F32),
            jax.ShapeDtypeStruct(top_rhs.shape, F32),
        ),
        in_specs=[smem, vmem, vmem, anywhere, anywhere, anywhere],
        out_specs=(vmem, vmem),
        scratch_shapes=[
            pltpu.VMEM((2, 8, 2, W1, HALF), F32),
            pltpu.VMEM((2, W1, 2 * HALF), BF16),
            pltpu.VMEM((BUFS, 2, 2, W2, W1), F32),
            pltpu.VMEM((NONE + 1, W2, HALF), F32),
            pltpu.VMEM((16, W2, HALF), F32),
            pltpu.VMEM((2, 16, W2, HALF), F32),
            pltpu.VMEM((2, 2, 6, CUT, HALF), F32),
            pltpu.VMEM((2, 2, 3, rest, HALF), F32),
            pltpu.VMEM((2, 8, rest, HALF), F32),
            pltpu.VMEM((2, 2, CUT, HALF), F32),
            pltpu.VMEM((2, W2, 2 * HALF), F32),
            pltpu.VMEM((2, W2, W2), F32),
            pltpu.VMEM((2, W2, W2), BF16),
            pltpu.VMEM((2, W2, W2), BF16),
            dma((BUFS,)),
            dma((2,)),
            dma((2, 2, 5)),
            dma((2, 2, 5)),
            dma((2, 2, 2)),
            dma((2, 2, 2)),
            dma((16,)),
            dma((2, 16)),
            dma((2, 2, 6)),
            dma((2, 2, 6)),
            dma((2, 2, 3)),
            dma((2, 2, 3)),
            dma((2, 8)),
            dma((2, 8)),
            dma((2, 2)),
            dma((2, 2)),
        ],
        compiler_params=pltpu.CompilerParams(
            collective_id=0, has_side_effects=True, vmem_limit_bytes=60 * 1024 * 1024
        ),
        cost_estimate=pl.CostEstimate(flops=7_500_000_000, bytes_accessed=40_000_000, transcendentals=0),
    )(meta, leaf_rhs, leaf_inverse, off_blocks, top_rhs, top_inverse)


def solution(mesh):
    return jax.shard_map(
        per_device,
        mesh=mesh,
        in_specs=(
            P("prow", "pcol", None, None),
            P("prow", "pcol", None, None),
            P("prow", None, None, "pcol", None, None),
            P("prow", None, None, "pcol"),
            P("prow", None, None, "pcol"),
            P(("prow", "pcol"), None, None),
            P(("prow", "pcol"), None, None),
        ),
        out_specs=(P("prow", "pcol", None, None), P(("prow", "pcol"), None, None)),
        check_vma=False,
    )
```

time: 366 us -> 118 us (0.32)
  waiting for transfers between devices: 240 us -> 0 us
  Pallas kernels: 0 us -> 111 us
  matrix products: 75 us -> 0 us
  local copies, waits for them, and re-layouts: 35.5 us -> 4.68 us
  between operations: 14.1 us -> 0.73 us
    reduce_scatter x1 -> x0, waiting for transfers between devices: 147 us -> none  [solve_columns(): lax.psum_scatter(partial_update, 'pcol', scatter_dimension=0, tiled=True)]
    pallas_call x0 -> x1, Pallas kernels: none -> 111 us  [per_device(): pl.pallas_call(kernel, out_shape=(jax.ShapeDtypeStruct(leaf_rhs.shape, F3...]
    all_gather x1 -> x0, waiting for transfers between devices: 92.4 us -> none  [gather_pieces(): return lax.all_gather(solved, 'prow', axis=0, tiled=True)]
    dot_general x4 -> x0, matrix products: 75 us -> none  [the longest x1 34.5 us: block_terms(): jnp.einsum('auvij,uvjr->auvir', blocks, pieces, precision=lax.Precision.H...]
    transpose x1 -> x0, local copies, waits for them, and re-layouts: 17.4 us -> none  [block_terms(): jnp.einsum('auvij,uvjr->auvir', blocks, pieces, precision=lax.Precision.H...]
    dot_general x1 -> x0, local copies, waits for them, and re-layouts: 15.8 us -> none  [spread_rows(): jnp.dot(choose, flat, precision=lax.Precision.HIGHEST, preferred_element_...]
  transfers between devices with their start and end apart: 2 -> 0, of which waited for: 2 -> 0; matrix products, arithmetic and copies ran while one was open for 0% -> 0% of each run, Pallas kernels for 0% -> 0%
where the time goes in v1:
time: 118 us
  Pallas kernels  111 us (94%)
  local copies, waits for them, and re-layouts  4.68 us (4%)
  other arithmetic  1.58 us (1%)
    pallas_call x1, Pallas kernels, per_device(): pl.pallas_call(kernel, out_shape=(jax.ShapeDtypeStruct(leaf_rhs.shape, F3...  111 us
    unnamed x2, local copies, waits for them, and re-layouts  4.13 us

profile of v1, /device:TPU:1, one launch (start us, length us, event | category | flops | bytes accessed | tf_op | source)
XLA Modules:
  0.0 118.0 jit_solution(13869493040361788491)
XLA Ops:
  0.7 0.7 compare_select_fusion
  1.4 0.1 copy.11
  1.5 0.1 select_n.84
  1.6 0.1 pad_add_fusion
  1.7 0.1 subtract_add_fusion
  1.7 0.1 reshape.134
  1.8 0.1 broadcast_select_fusion
  1.9 0.1 select_n.89
  2.0 0.1 iota.51
  2.1 0.1 iota.53
  2.2 0.1 select_reduce_fusion
  2.3 0.5 compare_select_fusion.1.meta
  2.9 111.0 %shard_map.86 = (f32[1,2,256,256]{3,2,1,0:T(8,128)}, f32[2,512,256]{2,1,0:T(8,128)}) custom-call(s32[64]{0:T(128)} %compare_select_fusion.1.meta, f32[1,2,256,256]{3,2,1,0:T(8,128)} %leaf_rhs.1, f32[1,2,256,256]{3,2,1,0:T(8,128)} %leaf_inv.1, f32[1,2,8,2,512,256]{5,4,3,2,1,0:T(8,128)} %off_blocks.1, f32[2,512,256]{2,1,0:T(8,128)} %top_rhs.1, ...), custom_call_target="tpu_custom_call" | custom-call | flops 7500000256 | bytes 40000000 | tf_op jit(solution)/shard_map/pallas_call | solution.py:361
  113.9 1.9 %copy.14 = f32[1,2,256,256]{3,2,1,0:T(8,128)} copy(f32[1,2,256,256]{3,2,1,0:T(8,128)} %get-tuple-element.8) | data formatting | bytes 1048576
  115.8 2.3 %copy.15 = f32[2,512,256]{2,1,0:T(8,128)} copy(f32[2,512,256]{2,1,0:T(8,128)} %get-tuple-element.9) | data formatting | bytes 2097152
  (10 shorter events, 0.1 us)

commit v2 on v1

v2 whole, which is shorter than its diff:
```python
import jax
import jax.numpy as jnp
from jax import lax
from jax.experimental import pallas as pl
from jax.experimental.pallas import tpu as pltpu
from jax.sharding import PartitionSpec as P

MESH = pl.DeviceIdType.MESH
F32, BF16 = jnp.float32, jnp.bfloat16
W1, W2, HALF = 256, 512, 128
STEPS = 8
BUFS = 3
CUT = 288
NONE = 32

UNITS = (
    (1, 2, 0), (1, 2, 1), (0, 2, 0), (0, 2, 1),
    (1, 1, 1), (1, 3, 0), (0, 1, 1), (0, 3, 0),
    (1, 1, 0), (1, 3, 1), (0, 1, 0), (0, 3, 1),
    (1, 0, 0), (1, 0, 1), (0, 0, 0), (0, 0, 1),
)
Y_SEND = ((0, 2, 4, 6, 8, 10), (1, 3, 5, 7, 9, 11))
Y_ADD = ((8, 10, 13, 15, 12, 14), (9, 11, 12, 14, 13, 15))
X_SEND = (0, 1, 4, 5, 8, 9, 12, 13)
XY_SEND = ((2, 6, 10), (3, 7, 11))
XY_ADD = ((10, 15, 14), (11, 14, 15))


ORDER = (
    ("leaf", 0), ("own", 0), ("leaf", 1), ("p", 0, 0), ("inv",), ("zpass", 0, 0), ("zpass", 0, 1), ("near", 0, 0),
    ("near", 0, 1), ("p", 0, 1), ("p", 0, 2), ("p", 0, 3), ("far", 0), ("own", 1), ("p", 0, 4), ("p", 0, 5),
    ("p", 0, 6), ("p", 0, 7), ("zpass", 1, 0), ("zpass", 1, 1), ("give", 0, 0), ("give", 0, 1), ("give", 0, 2),
    ("give", 0, 3), ("give", 0, 4), ("give", 0, 5), ("give", 0, 6), ("give", 0, 7), ("give", 0, 8), ("give", 0, 9),
    ("give", 0, 10), ("give", 0, 11), ("give", 0, 12), ("give", 0, 13), ("give", 0, 14), ("near", 1, 0),
    ("give", 0, 15), ("sum", 0, 0), ("sum", 0, 1), ("sum", 0, 2), ("sum", 0, 3), ("near", 1, 1), ("sum", 0, 4),
    ("sum", 0, 5), ("sum", 0, 6), ("sum", 0, 7), ("sum", 0, 8), ("sum", 0, 9), ("xadd", 0, 0), ("far", 1, 0),
    ("sum", 0, 10), ("ypass", 0, 0, 0), ("sum", 0, 11), ("ypass", 0, 1, 0), ("sum", 0, 12), ("sum", 0, 13),
    ("xadd", 0, 1), ("sum", 0, 14), ("sum", 0, 15), ("far", 1, 1), ("p", 1, 0), ("ypass", 0, 0, 1), ("p", 1, 1),
    ("ypass", 0, 1, 1), ("xadd", 0, 2), ("p", 1, 2), ("p", 1, 3), ("xadd", 0, 3), ("p", 1, 4), ("p", 1, 5),
    ("xadd", 0, 4), ("p", 1, 6), ("p", 1, 7), ("give", 1, 0), ("give", 1, 1), ("xadd", 0, 5), ("give", 1, 2),
    ("give", 1, 3), ("xypass", 0, 0), ("give", 1, 4), ("give", 1, 5), ("give", 1, 6), ("give", 1, 7), ("give", 1, 8),
    ("give", 1, 9), ("give", 1, 10), ("give", 1, 11), ("give", 1, 12), ("give", 1, 13), ("ylast", 0, 1),
    ("give", 1, 14), ("give", 1, 15), ("xadd", 0, 6), ("sum", 1, 0), ("sum", 1, 1), ("ylast", 0, 0), ("sum", 1, 2),
    ("xypass", 0, 1), ("sum", 1, 3), ("sum", 1, 4), ("xadd", 0, 7), ("sum", 1, 5), ("sum", 1, 6), ("sum", 1, 7),
    ("sum", 1, 8), ("sum", 1, 9), ("sum", 1, 10), ("sum", 1, 11), ("sum", 1, 12), ("sum", 1, 13), ("sum", 1, 14),
    ("sum", 1, 15), ("xadd", 1, 0), ("ypass", 1, 1, 0), ("xadd", 1, 1), ("ypass", 1, 0, 0), ("fin", 0, 1),
    ("fin", 0, 0), ("ypass", 1, 0, 1), ("ypass", 1, 1, 1), ("xadd", 1, 2), ("xadd", 1, 3), ("xadd", 1, 4),
    ("xadd", 1, 5), ("xypass", 1, 0), ("ylast", 1, 1), ("xadd", 1, 6), ("ylast", 1, 0), ("xypass", 1, 1),
    ("xadd", 1, 7), ("fin", 1, 0), ("fin", 1, 1),
)


def split(value):
    high = value.astype(BF16)
    return high, (value - high.astype(F32)).astype(BF16)


def dot(a, b):
    return jnp.dot(a, b, preferred_element_type=F32)


def times(a_high, a_low, both, high):
    wide = dot(a_high, both)
    return wide[:, :HALF] + wide[:, HALF:] + dot(a_low, high)


def kernel(
    meta, leaf_rhs, leaf_inv, off_blocks, top_rhs, top_inv, leaf_out, top_out,
    x, w, blocks, chain, give, s, yr, xyr, xr, x2r, rhs, inv, inv_high, inv_low,
    block_sem, top_sem, az_s, az_r, ax_s, ax_r, core_s, core_r, y_s, y_r, xy_s, xy_r, x_s, x_r, x2_s, x2_r,
):
    row, col = lax.axis_index("prow"), lax.axis_index("pcol")
    z, xl = row // 2, row % 2
    xh, y, core = col // 8, (col // 2) % 4, col % 2

    def rows_at(dz, dx):
        return ((z + dz) % 4) * 2 + (xl + dx) % 2

    def at(dxh, dy, dcore):
        return ((xh + dxh) % 2) * 8 + ((y + dy) % 4) * 2 + (core + dcore) % 2

    x_near = (rows_at(0, 1), col)
    z_to = ((rows_at(1, 0), col), (rows_at(3, 0), col))
    other_core = (row, at(0, 0, 1))
    x_far = (row, at(1, 0, 0))
    y_to = ((row, at(0, 1, 0)), (row, at(0, 3, 0)))
    order = [rows_at(*d) for d in ((0, 0), (0, 1), (3, 0), (1, 0), (2, 0), (3, 1), (1, 1), (2, 1))]

    def send(src, dst, send_sem, recv_sem, device):
        return pltpu.make_async_remote_copy(
            src_ref=src, dst_ref=dst, send_sem=send_sem, recv_sem=recv_sem, device_id=device, device_id_type=MESH
        )

    def fetch(g):
        u = order[g % STEPS]
        return pltpu.make_async_copy(off_blocks.at[0, :, u], blocks.at[g % BUFS], block_sem.at[g % BUFS])

    for g in range(BUFS):
        fetch(g).start()
    fetch_rhs = pltpu.make_async_copy(top_rhs, rhs, top_sem.at[0])
    fetch_inv = pltpu.make_async_copy(top_inv, inv, top_sem.at[1])
    fetch_rhs.start()
    fetch_inv.start()

    barrier = pltpu.get_barrier_semaphore()
    partners = (x_near, *z_to, other_core, x_far, *y_to)
    for partner in partners:
        pl.semaphore_signal(barrier, inc=1, device_id=partner, device_id_type=MESH)

    chain[NONE] = jnp.zeros((W2, HALF), F32)

    started, seen = {}, set()

    def put(key):
        started[key] = message(*key)
        started[key].start()

    def need(*keys):
        for key in keys:
            if key not in seen:
                seen.add(key)
                message(*key).wait_recv()

    def message(kind, ch, j, k=0):
        low, high = pl.ds(0, CUT), pl.ds(CUT, W2 - CUT)
        if kind == "near":
            ref = x.at[ch, order[0] if j == 0 else order[4], k]
            return send(ref, ref, ax_s.at[ch, j, k], ax_r.at[ch, j, k], x_near)
        if kind == "z":
            u = (order[0], order[0], order[2 + j], order[1], order[1], order[5 + j])[k]
            ref = x.at[ch, u, (j, 1 - j, j, 0, 1, j)[k]]
            return send(ref, ref, az_s.at[ch, j, k], az_r.at[ch, j, k], z_to[j])
        if kind == "core":
            return send(give.at[j], s.at[ch, j], core_s.at[j], core_r.at[ch, j], other_core)
        if kind == "y":
            return send(s.at[ch, Y_SEND[j][k], low], yr.at[ch, j, k], y_s.at[ch, j, k], y_r.at[ch, j, k], y_to[j])
        if kind == "xy":
            return send(s.at[ch, XY_SEND[j][k], high], xyr.at[ch, j, k], xy_s.at[ch, j, k], xy_r.at[ch, j, k], y_to[j])
        if kind == "x":
            return send(s.at[ch, X_SEND[j], high], xr.at[ch, j], x_s.at[ch, j], x_r.at[ch, j], x_far)
        return send(s.at[ch, 12 + j, low], x2r.at[ch, j], x2_s.at[ch, j], x2_r.at[ch, j], x_far)

    def leaf(ch):
        cols = slice(ch * HALF, (ch + 1) * HALF)
        for v in range(2):
            i_high, i_low = split(leaf_inv[0, v])
            r_high, r_low = split(leaf_rhs[0, v, :, cols])
            solved = times(i_high, i_low, jnp.concatenate([r_high, r_low], axis=1), r_high)
            x[ch, row, v] = solved
            leaf_out[0, v, :, cols] = solved

    def own(ch):
        if ch == 0:
            pl.semaphore_wait(barrier, len(partners))
        for j in range(2):
            put(("near", ch, 0, j))
            for d in range(2):
                put(("z", ch, d, j))

    def zpass(ch, d):
        need(("z", ch, d, 0))
        put(("z", ch, d, 2))

    def near(ch, j):
        need(("near", ch, 0, j))
        for d in range(2):
            put(("z", ch, d, 3 + j))

    def far(ch, d=0):
        if ch == 0:
            need(("z", ch, 0, 2), ("z", ch, 1, 2))
            for v in range(2):
                put(("near", ch, 1, v))
        else:
            need(("z", ch, d, 3 + d))
            put(("z", ch, d, 5))

    def products(ch, step):
        last = [("near", 0, 1, 0), ("near", 0, 1, 1)] if ch == 0 else [("z", 1, 0, 5), ("z", 1, 1, 5)]
        need(
            *(
                [],
                [("near", ch, 0, 0), ("near", ch, 0, 1)],
                [("z", ch, 0, 0), ("z", ch, 0, 1)],
                [("z", ch, 1, 0), ("z", ch, 1, 1)],
                [("z", ch, 0, 2), ("z", ch, 1, 2)],
                [("z", ch, 0, 3), ("z", ch, 0, 4)],
                [("z", ch, 1, 3), ("z", ch, 1, 4)],
                last,
            )[step]
        )
        g = ch * STEPS + step
        u = order[step]
        fetch(g).wait()
        for v in range(2):
            high, low = split(x[ch, u, v])
            w[v, :, :HALF] = high
            w[v, :, HALF:] = low

        def one(v, carry):
            for a in range(2):
                before = meta[a * 16 + u * 2 + v]
                for tile in range(2):
                    tall = slice(tile * 256, tile * 256 + 256)
                    b_high, b_low = split(blocks[g % BUFS, a, v, tall, :])
                    term = times(b_high, b_low, w[v], w[v, :, :HALF])
                    chain[step * 4 + v * 2 + a, tall, :] = term + chain[before, tall, :]
            return carry

        lax.fori_loop(0, 2, one, 0)
        if g + BUFS < 2 * STEPS:
            fetch(g + BUFS).start()

    def number(i, its_core):
        dxh, dy, e = UNITS[i]
        return ((xh + dxh) % 2) * 16 + ((y + dy) % 4) * 4 + its_core * 2 + e

    def share_core(ch, i):
        if ch:
            started.pop(("core", 0, i)).wait_send()
        give[i] = chain[meta[32 + number(i, 1 - core)]]
        put(("core", ch, i))

    def sum_core(ch, i):
        need(("core", ch, i))
        s[ch, i] = s[ch, i] + chain[meta[32 + number(i, core)]]
        for d in range(2):
            if i in Y_SEND[d][:4]:
                put(("y", ch, d, Y_SEND[d].index(i)))
        if i in X_SEND:
            put(("x", ch, X_SEND.index(i)))

    def y_add(ch, i, least):
        for d in range(2):
            for j in range(least, 6):
                if Y_ADD[d][j] == i:
                    need(("y", ch, d, j))
                    s[ch, i, :CUT] = s[ch, i, :CUT] + yr[ch, d, j]

    def y_pass(ch, d, j):
        need(("y", ch, d, j))
        i = Y_ADD[d][j]
        s[ch, i, :CUT] = s[ch, i, :CUT] + yr[ch, d, j]
        put(("y", ch, d, 4 + j))

    def x_add(ch, m):
        need(("x", ch, m))
        i = X_SEND[m] + 2
        s[ch, i, CUT:] = s[ch, i, CUT:] + xr[ch, m]
        for d in range(2):
            if i in XY_SEND[d][:2]:
                put(("xy", ch, d, XY_SEND[d].index(i)))

    def xy_pass(ch, d):
        need(("xy", ch, d, 0))
        i = XY_ADD[d][0]
        s[ch, i, CUT:] = s[ch, i, CUT:] + xyr[ch, d, 0]
        put(("xy", ch, d, 2))

    def y_last(ch, e):
        y_add(ch, 12 + e, 2)
        put(("last", ch, e))

    def split_inv():
        fetch_rhs.wait()
        fetch_inv.wait()

        def one(i, carry):
            e, tall = i // 4, pl.ds(pl.multiple_of((i % 4) * 128, 128), 128)
            high, low = split(inv[e, tall, :])
            inv_high[e, tall, :] = high
            inv_low[e, tall, :] = low
            return carry

        lax.fori_loop(0, 8, one, 0)

    def finish(ch, e):
        i = 14 + e
        y_add(ch, i, 2)
        for d in range(2):
            for j in (1, 2):
                if XY_ADD[d][j] == i:
                    need(("xy", ch, d, j))
                    s[ch, i, CUT:] = s[ch, i, CUT:] + xyr[ch, d, j]
        need(("last", ch, e))
        s[ch, i, :CUT] = s[ch, i, :CUT] + x2r[ch, e]
        cols = slice(ch * HALF, (ch + 1) * HALF)
        high, low = split(rhs[e, :, cols] - s[ch, i])
        both = jnp.concatenate([high, low], axis=1)
        top_out[e, :256, cols] = times(inv_high[e, :256, :256], inv_low[e, :256, :256], both[:256], high[:256])
        top_out[e, 256:, cols] = times(inv_high[e, 256:], inv_low[e, 256:], both, high)

    tasks = {
        "leaf": leaf, "own": own, "zpass": zpass, "near": near, "far": far, "p": products, "inv": split_inv,
        "give": share_core, "sum": sum_core, "ypass": y_pass, "xadd": x_add, "xypass": xy_pass,
        "ylast": y_last, "fin": finish,
    }
    for name, *numbers in ORDER:
        tasks[name](*numbers)
    for copy in started.values():
        copy.wait_send()


def hand_over(leaf_in, top_in, leaf_out, top_out, leaf, top, sem):
    pieces = [(ref.at[0, v], held.at[0, v], out.at[0, v]) for ref, held, out in ((leaf_in, leaf, leaf_out),) for v in range(2)]
    pieces += [
        (top_in.at[e, half], top.at[e, half], top_out.at[e, half])
        for e in range(2)
        for half in (pl.ds(0, 256), pl.ds(256, 256))
    ]
    loads = [pltpu.make_async_copy(src, held, sem.at[0, i]) for i, (src, held, _) in enumerate(pieces)]
    stores = [pltpu.make_async_copy(held, out, sem.at[1, i]) for i, (_, held, out) in enumerate(pieces)]
    for load in loads:
        load.start()
    for load, store in zip(loads, stores):
        load.wait()
        store.start()
    for store in stores:
        store.wait()


def chains(rows_index, present, row):
    u = lax.broadcasted_iota(jnp.int32, (2, 8, 2), 1)
    a = lax.broadcasted_iota(jnp.int32, (2, 8, 2), 0)
    v = lax.broadcasted_iota(jnp.int32, (2, 8, 2), 2)
    far = (u // 2 - row // 2 + 4) % 4
    near = (u + row) % 2
    step = jnp.where(
        far == 0, near, jnp.where(far == 3, 2 + 3 * near, jnp.where(far == 1, 3 + 3 * near, 4 + 3 * near))
    )
    rank = (step * 4 + v * 2 + a).reshape(-1)
    wanted = jnp.where(present != 0, rows_index, -1).reshape(-1)
    ask = jnp.concatenate([wanted, jnp.arange(32, dtype=jnp.int32)])
    limit = jnp.concatenate([rank, jnp.full((32,), 32, jnp.int32)])
    fits = (wanted[None, :] == ask[:, None]) & (rank[None, :] < limit[:, None])
    found = jnp.max(jnp.where(fits, rank[None, :], -1), axis=1)
    return jnp.where(found < 0, NONE, found)


def per_device(leaf_rhs, leaf_inverse, off_blocks, ancestor_rows, block_present, top_rhs, top_inverse):
    meta = chains(ancestor_rows[0], block_present[0], lax.axis_index("prow"))
    vmem = pl.BlockSpec(memory_space=pltpu.VMEM)
    smem = pl.BlockSpec(memory_space=pltpu.SMEM)
    anywhere = pl.BlockSpec(memory_space=pl.ANY)
    rest = W2 - CUT
    dma = pltpu.SemaphoreType.DMA
    leaf, top = pl.pallas_call(
        kernel,
        out_shape=(
            jax.ShapeDtypeStruct(leaf_rhs.shape, F32),
            jax.ShapeDtypeStruct(top_rhs.shape, F32),
        ),
        in_specs=[smem, vmem, vmem, anywhere, anywhere, anywhere],
        out_specs=(vmem, vmem),
        scratch_shapes=[
            pltpu.VMEM((2, 8, 2, W1, HALF), F32),
            pltpu.VMEM((2, W1, 2 * HALF), BF16),
            pltpu.VMEM((BUFS, 2, 2, W2, W1), F32),
            pltpu.VMEM((NONE + 1, W2, HALF), F32),
            pltpu.VMEM((16, W2, HALF), F32),
            pltpu.VMEM((2, 16, W2, HALF), F32),
            pltpu.VMEM((2, 2, 6, CUT, HALF), F32),
            pltpu.VMEM((2, 2, 3, rest, HALF), F32),
            pltpu.VMEM((2, 8, rest, HALF), F32),
            pltpu.VMEM((2, 2, CUT, HALF), F32),
            pltpu.VMEM((2, W2, 2 * HALF), F32),
            pltpu.VMEM((2, W2, W2), F32),
            pltpu.VMEM((2, W2, W2), BF16),
            pltpu.VMEM((2, W2, W2), BF16),
            dma((BUFS,)),
            dma((2,)),
            dma((2, 2, 6)),
            dma((2, 2, 6)),
            dma((2, 2, 2)),
            dma((2, 2, 2)),
            dma((16,)),
            dma((2, 16)),
            dma((2, 2, 6)),
            dma((2, 2, 6)),
            dma((2, 2, 3)),
            dma((2, 2, 3)),
            dma((2, 8)),
            dma((2, 8)),
            dma((2, 2)),
            dma((2, 2)),
        ],
        compiler_params=pltpu.CompilerParams(
            collective_id=0, has_side_effects=True, vmem_limit_bytes=60 * 1024 * 1024
        ),
        cost_estimate=pl.CostEstimate(flops=7_500_000_000, bytes_accessed=40_000_000, transcendentals=0),
    )(meta, leaf_rhs, leaf_inverse, off_blocks, top_rhs, top_inverse)
    return pl.pallas_call(
        hand_over,
        out_shape=(jax.ShapeDtypeStruct(leaf_rhs.shape, F32), jax.ShapeDtypeStruct(top_rhs.shape, F32)),
        in_specs=[anywhere, anywhere],
        out_specs=(anywhere, anywhere),
        scratch_shapes=[pltpu.VMEM(leaf_rhs.shape, F32), pltpu.VMEM(top_rhs.shape, F32), dma((2, 6))],
    )(leaf, top)


def solution(mesh):
    return jax.shard_map(
        per_device,
        mesh=mesh,
        in_specs=(
            P("prow", "pcol", None, None),
            P("prow", "pcol", None, None),
            P("prow", None, None, "pcol", None, None),
            P("prow", None, None, "pcol"),
            P("prow", None, None, "pcol"),
            P(("prow", "pcol"), None, None),
            P(("prow", "pcol"), None, None),
        ),
        out_specs=(P("prow", "pcol", None, None), P(("prow", "pcol"), None, None)),
        check_vma=False,
    )
```

time: 118 us -> 95.2 us (0.81)
  Pallas kernels: 111 us -> 92 us
  local copies, waits for them, and re-layouts: 4.68 us -> 0.55 us
    pallas_call x1, Pallas kernels: 111 us -> 89.8 us  [per_device(): pl.pallas_call(kernel, out_shape=(jax.ShapeDtypeStruct(leaf_rhs.shape, F3...]
    unnamed x2 -> x0, local copies, waits for them, and re-layouts: 4.13 us -> none
    pallas_call x0 -> x1, Pallas kernels: none -> 2.19 us  [per_device(): pl.pallas_call(hand_over, out_shape=(jax.ShapeDtypeStruct(leaf_rhs.shape,...]
where the time goes in v2:
time: 95.2 us; the launch traced here: 95 us
  Pallas kernels  92 us (97%)
  other arithmetic  1.58 us (2%)
    pallas_call x1, Pallas kernels, per_device(): pl.pallas_call(kernel, out_shape=(jax.ShapeDtypeStruct(leaf_rhs.shape, F3...  89.8 us
    pallas_call x1, Pallas kernels, per_device(): pl.pallas_call(hand_over, out_shape=(jax.ShapeDtypeStruct(leaf_rhs.shape,...  2.19 us

profile of v2, /device:TPU:1, one launch (start us, length us, event | category | flops | bytes accessed | tf_op | source)
XLA Modules:
  0.0 95.0 jit_solution(5221927772975047981)
XLA Ops:
  0.7 0.7 compare_select_fusion
  1.4 0.1 copy.11
  1.5 0.1 select_n.84
  1.6 0.1 pad_add_fusion
  1.7 0.1 subtract_add_fusion
  1.7 0.1 reshape.134
  1.8 0.1 broadcast_select_fusion
  1.9 0.1 select_n.89
  2.0 0.1 iota.51
  2.1 0.1 iota.53
  2.2 0.1 select_reduce_fusion
  2.3 0.5 compare_select_fusion.1.meta
  2.9 89.8 %shard_map.86 = (f32[1,2,256,256]{3,2,1,0:T(8,128)}, f32[2,512,256]{2,1,0:T(8,128)}) custom-call(s32[64]{0:T(128)} %compare_select_fusion.1.meta, f32[1,2,256,256]{3,2,1,0:T(8,128)} %leaf_rhs.1, f32[1,2,256,256]{3,2,1,0:T(8,128)} %leaf_inv.1, f32[1,2,8,2,512,256]{5,4,3,2,1,0:T(8,128)} %off_blocks.1, f32[2,512,256]{2,1,0:T(8,128)} %top_rhs.1, ...), custom_call_target="tpu_custom_call" | custom-call | flops 7500000256 | bytes 40000000 | tf_op jit(solution)/shard_map/pallas_call | solution.py:347
  92.7 2.2 %shard_map.87 = (f32[1,2,256,256]{3,2,1,0:T(8,128)}, f32[2,512,256]{2,1,0:T(8,128)}) custom-call(f32[1,2,256,256]{3,2,1,0:T(8,128)} %get-tuple-element.4.leaf_in, f32[2,512,256]{2,1,0:T(8,128)} %get-tuple-element.5.top_in), custom_call_target="tpu_custom_call" | custom-call | tf_op jit(solution)/shard_map/pallas_call | solution.py:392
  (10 shorter events, 0.1 us)

commit v3 on v2

v3 whole, which is shorter than its diff:
```python
import jax
import jax.numpy as jnp
from jax import lax
from jax.experimental import pallas as pl
from jax.experimental.pallas import tpu as pltpu
from jax.sharding import PartitionSpec as P

MESH = pl.DeviceIdType.MESH
F32, BF16 = jnp.float32, jnp.bfloat16
W1, W2, HALF = 256, 512, 128
STEPS = 8
BUFS = 3
CUT = 320
REST = W2 - CUT
NONE = 32
PACKED = (True, True, False)
PARTS = len(PACKED)
NARROW = tuple(c for c in range(PARTS) if PACKED[c])
CHAINS = 2
FAR_BY_Z = (False, True, True)

UNITS = (
    (1, 2, 0), (1, 2, 1), (0, 2, 0), (0, 2, 1),
    (1, 1, 1), (1, 3, 0), (0, 1, 1), (0, 3, 0),
    (1, 1, 0), (1, 3, 1), (0, 1, 0), (0, 3, 1),
    (1, 0, 0), (1, 0, 1), (0, 0, 0), (0, 0, 1),
)
PAIRS = ((1, 2), (0, 2), (1, 1), (1, 3), (0, 1), (0, 3), (1, 0), (0, 0))
Y_SEND = ((0, 2, 4, 6, 8, 10), (1, 3, 5, 7, 9, 11))
Y_ADD = ((8, 10, 13, 15, 12, 14), (9, 11, 12, 14, 13, 15))
X_SEND = (0, 1, 4, 5, 8, 9, 12, 13)
XY_SEND = ((2, 6, 10), (3, 7, 11))
XY_ADD = ((10, 15, 14), (11, 14, 15))


ORDER = (
    ("leaf", 0), ("own", 0), ("chains",), ("leaf", 2), ("p", 0, 0), ("inv",), ("zpass", 0, 0), ("zpass", 0, 1),
    ("near", 0, 0), ("near", 0, 1), ("p", 0, 1), ("p", 0, 2), ("far", 0, 0), ("far", 0, 1), ("own", 1), ("p", 0, 3),
    ("p", 0, 4), ("p", 0, 5), ("p", 0, 6), ("zpass", 1, 1), ("zpass", 1, 0), ("p", 0, 7), ("give", 0, 0),
    ("give", 0, 1), ("give", 0, 2), ("near", 1, 0), ("give", 0, 3), ("give", 0, 4), ("p", 1, 0), ("near", 1, 1),
    ("p", 1, 1), ("sum", 0, 0), ("p", 1, 2), ("far", 1, 0), ("sum", 0, 1), ("p", 1, 3), ("far", 1, 1), ("own", 2),
    ("sum", 0, 2), ("sum", 0, 3), ("sum", 0, 4), ("give", 0, 5), ("give", 0, 6), ("give", 0, 7), ("xadd", 0, 0),
    ("p", 1, 4), ("p", 1, 5), ("ypass", 0, 0, 1), ("xadd", 0, 1), ("ypass", 0, 0, 0), ("sum", 0, 5),
    ("ypass", 0, 1, 1), ("p", 1, 6), ("p", 1, 7), ("give", 1, 0), ("sum", 0, 6), ("sum", 0, 7), ("near", 2, 0),
    ("p", 2, 0), ("give", 1, 1), ("give", 1, 2), ("zpass", 2, 0), ("ypass", 0, 1, 0), ("p", 2, 1), ("xadd", 0, 2),
    ("near", 2, 1), ("sum", 1, 0), ("give", 1, 3), ("zpass", 2, 1), ("p", 2, 2), ("sum", 1, 1), ("p", 2, 3),
    ("xadd", 0, 3), ("xadd", 0, 4), ("xypass", 0, 0), ("far", 2, 0), ("ylast", 0, 1), ("xadd", 0, 5),
    ("xypass", 0, 1), ("ylast", 0, 0), ("sum", 1, 2), ("sum", 1, 3), ("give", 1, 4), ("give", 1, 5), ("give", 1, 6),
    ("give", 1, 7), ("xadd", 0, 6), ("ypass", 1, 1, 0), ("ypass", 1, 0, 0), ("xadd", 0, 7), ("far", 2, 1),
    ("xadd", 1, 0), ("sum", 1, 4), ("ypass", 1, 0, 1), ("sum", 1, 5), ("xadd", 1, 1), ("ypass", 1, 1, 1),
    ("sum", 1, 6), ("sum", 1, 7), ("p", 2, 4), ("p", 2, 5), ("p", 2, 6), ("p", 2, 7), ("give", 2, 0),
    ("ylast", 1, 1), ("xadd", 1, 2), ("xadd", 1, 4), ("xypass", 1, 0), ("give", 2, 1), ("give", 2, 2),
    ("give", 2, 3), ("give", 2, 4), ("give", 2, 5), ("fin", 0, 0), ("xadd", 1, 3), ("give", 2, 6), ("give", 2, 7),
    ("give", 2, 8), ("give", 2, 9), ("give", 2, 10), ("give", 2, 11), ("give", 2, 12), ("give", 2, 13),
    ("give", 2, 14), ("give", 2, 15), ("xadd", 1, 5), ("xypass", 1, 1), ("ylast", 1, 0), ("sum", 2, 0),
    ("fin", 0, 1), ("xadd", 1, 6), ("sum", 2, 1), ("sum", 2, 2), ("sum", 2, 3), ("xadd", 1, 7), ("sum", 2, 4),
    ("sum", 2, 5), ("sum", 2, 6), ("fin", 1, 1), ("sum", 2, 7), ("sum", 2, 8), ("sum", 2, 9), ("fin", 1, 0),
    ("sum", 2, 10), ("top", 0, 1), ("ypass", 2, 0, 0), ("sum", 2, 11), ("sum", 2, 12), ("top", 0, 0),
    ("ypass", 2, 1, 0), ("sum", 2, 13), ("sum", 2, 14), ("xadd", 2, 0), ("sum", 2, 15), ("xadd", 2, 1),
    ("ypass", 2, 0, 1), ("ypass", 2, 1, 1), ("xadd", 2, 2), ("xadd", 2, 3), ("xadd", 2, 4), ("xadd", 2, 5),
    ("xadd", 2, 6), ("ylast", 2, 0), ("ylast", 2, 1), ("xadd", 2, 7), ("xypass", 2, 0), ("xypass", 2, 1),
    ("fin", 2, 0), ("top", 1, 0), ("fin", 2, 1), ("top", 1, 1),
)

def split(value):
    high = value.astype(BF16)
    return high, (value - high.astype(F32)).astype(BF16)


def dot(a, b):
    return jnp.dot(a, b, preferred_element_type=F32)


def times(a_high, a_low, both, high):
    wide = dot(a_high, both)
    return wide[:, :HALF] + wide[:, HALF:] + dot(a_low, high)


def kernel(
    wanted, leaf_rhs_in, leaf_inv_in, off_blocks, top_rhs, top_inv, leaf_to, top_to,
    leaf_rhs, leaf_inv, leaf_out, top_out, found, meta,
    x_wide, x_pack, w, blocks, chain, give, s_wide, s_pack, y_wide, y_pack, xy_wide, xy_pack, far_wide, far_pack,
    last_wide, last_pack, rhs, inv, inv_high, inv_low,
    block_sem, top_sem, leaf_sem, out_sem, meta_sem, az_s, az_r, ax_s, ax_r, core_s, core_r, y_s, y_r, xy_s, xy_r, x_s, x_r, x2_s, x2_r,
):
    row, col = lax.axis_index("prow"), lax.axis_index("pcol")
    z, xl = row // 2, row % 2
    xh, y, core = col // 8, (col // 2) % 4, col % 2

    def rows_at(dz, dx):
        return ((z + dz) % 4) * 2 + (xl + dx) % 2

    def at(dxh, dy, dcore):
        return ((xh + dxh) % 2) * 8 + ((y + dy) % 4) * 2 + (core + dcore) % 2

    x_near = (rows_at(0, 1), col)
    z_to = ((rows_at(1, 0), col), (rows_at(3, 0), col))
    other_core = (row, at(0, 0, 1))
    x_far = (row, at(1, 0, 0))
    y_to = ((row, at(0, 1, 0)), (row, at(0, 3, 0)))
    order = [rows_at(*d) for d in ((0, 0), (0, 1), (3, 0), (1, 0), (2, 0), (3, 1), (1, 1), (2, 1))]

    def send(src, dst, send_sem, recv_sem, device):
        return pltpu.make_async_remote_copy(
            src_ref=src, dst_ref=dst, send_sem=send_sem, recv_sem=recv_sem, device_id=device, device_id_type=MESH
        )

    def fetch(g):
        u = order[g % STEPS]
        return pltpu.make_async_copy(off_blocks.at[0, :, u], blocks.at[g % BUFS], block_sem.at[g % BUFS])

    left = lax.broadcasted_iota(jnp.int32, (1, HALF), 1) < 64

    def beside(first, second):
        return jnp.where(left, first, second)

    def turn(value):
        return pltpu.roll(value, 64, 1)

    def solution_piece(c, u, k):
        if PACKED[c]:
            return x_pack.at[NARROW.index(c), u, pl.ds(k * 128, 128)]
        return x_wide.at[u, k]

    def band(c, i, high):
        if not PACKED[c]:
            return s_wide, (i, pl.ds(CUT, REST) if high else pl.ds(0, CUT))
        pair, k = PAIRS.index(UNITS[i][:2]), UNITS[i][2]
        rows = pl.ds(CUT + k * (REST // 2), REST // 2) if high else pl.ds(k * (CUT // 2), CUT // 2)
        return s_pack, (NARROW.index(c), pair, rows)

    def arrived(c, kind, *index):
        wide, pack = {"y": (y_wide, y_pack), "xy": (xy_wide, xy_pack), "x": (far_wide, far_pack), "last": (last_wide, last_pack)}[kind]
        return (pack, (NARROW.index(c), *index)) if PACKED[c] else (wide, index)

    def add(c, i, high, kind, *index):
        need((kind, c, *index))
        ref, at_rows = band(c, i, high)
        got, at_got = arrived(c, kind, *index)
        ref[at_rows] = ref[at_rows] + got[at_got]

    fetch_leaf = [
        pltpu.make_async_copy(src, dst, leaf_sem.at[i])
        for i, (src, dst) in enumerate(((leaf_inv_in, leaf_inv), (leaf_rhs_in, leaf_rhs)))
    ]
    for copy in fetch_leaf:
        copy.start()

    barrier = pltpu.get_barrier_semaphore()
    partners = (x_near, *z_to, other_core, x_far, *y_to)
    for partner in partners:
        pl.semaphore_signal(barrier, inc=1, device_id=partner, device_id_type=MESH)

    for g in range(BUFS):
        fetch(g).start()
    fetch_rhs = pltpu.make_async_copy(top_rhs, rhs, top_sem.at[0])
    fetch_inv = pltpu.make_async_copy(top_inv, inv, top_sem.at[1])
    fetch_rhs.start()
    fetch_inv.start()

    for k in range(CHAINS):
        chain[k, NONE] = jnp.zeros((W2, HALF), F32)

    for copy in fetch_leaf:
        copy.wait()

    started, seen = {}, set()

    def put(key):
        started[key] = message(*key)
        started[key].start()

    def need(*keys):
        for key in keys:
            if key not in seen:
                seen.add(key)
                message(*key).wait_recv()

    def message(kind, c, j, k=0):
        if kind == "near":
            ref = solution_piece(c, order[0] if j == 0 else order[4], k)
            return send(ref, ref, ax_s.at[c, j, k], ax_r.at[c, j, k], x_near)
        if kind == "z":
            u = (order[0], order[0], order[2 + j], order[1], order[1], order[5 + j])[k]
            ref = solution_piece(c, u, (j, 1 - j, j, 0, 1, j)[k])
            return send(ref, ref, az_s.at[c, j, k], az_r.at[c, j, k], z_to[j])
        if kind == "core":
            into = s_pack.at[NARROW.index(c), j] if PACKED[c] else s_wide.at[j]
            return send(give.at[j], into, core_s.at[c, j], core_r.at[c, j], other_core)
        if kind == "y":
            i, high, index, sems, device = Y_SEND[j][k], False, (j, k), (y_s, y_r), y_to[j]
        elif kind == "xy":
            i, high, index, sems, device = XY_SEND[j][k], True, (j, k), (xy_s, xy_r), y_to[j]
        elif kind == "x":
            i, high, index, sems, device = X_SEND[j], True, (j,), (x_s, x_r), x_far
        else:
            i, high, index, sems, device = 12 + j, False, (j,), (x2_s, x2_r), x_far
        src, at_src = band(c, i, high)
        dst, at_dst = arrived(c, kind, *index)
        return send(src.at[at_src], dst.at[at_dst], sems[0].at[(c, *index)], sems[1].at[(c, *index)], device)

    outs = []

    def out(src, dst, i):
        outs.append(pltpu.make_async_copy(src, dst, out_sem.at[i]))
        outs[-1].start()

    def solve(v, cols):
        i_high, i_low = split(leaf_inv[0, v])
        r_high, r_low = split(leaf_rhs[0, v, :, cols])
        solved = times(i_high, i_low, jnp.concatenate([r_high, r_low], axis=1), r_high)
        leaf_out[0, v, :, cols] = solved
        return solved

    def leaf(c):
        if PACKED[c]:
            first, second = solve(0, slice(0, HALF)), solve(1, slice(0, HALF))
            second = turn(second)
            x_pack[0, row] = beside(first, second)
            x_pack[1, row] = beside(second, first)
        else:
            for v in range(2):
                x_wide[row, v] = solve(v, slice(HALF, 2 * HALF))
            for v in range(2):
                out(leaf_out.at[0, v], leaf_to.at[0, v], v)

    def chains():
        lane = lax.broadcasted_iota(jnp.int32, (8, HALF), 1)
        ask, limit, slots = lane - 32, jnp.full((8, HALF), 32, jnp.int32), []
        for step in range(STEPS):
            for v in range(2):
                for a in range(2):
                    slot, b = step * 4 + v * 2 + a, a * 16 + order[step] * 2 + v
                    ask = jnp.where(lane == b, wanted[b], ask)
                    limit = jnp.where(lane == b, slot, limit)
                    slots.append((slot, wanted[b]))
        before = jnp.full((8, HALF), NONE, jnp.int32)
        for slot, its_row in slots:
            before = jnp.where((ask == its_row) & (limit > slot), slot, before)
        found[...] = before
        copy = pltpu.make_async_copy(found, meta, meta_sem.at[0])
        copy.start()
        copy.wait()

    def own(c):
        if c == 0:
            pl.semaphore_wait(barrier, len(partners))
        for j in range(2):
            put(("near", c, 0, j))
            for d in range(2):
                put(("z", c, d, j))

    def zpass(c, d):
        need(("z", c, d, 0))
        put(("z", c, d, 2))

    def near(c, j):
        need(("near", c, 0, j))
        for d in range(2):
            put(("z", c, d, 3 + j))

    def far(c, d):
        if FAR_BY_Z[c]:
            need(("z", c, d, 3 + d))
            put(("z", c, d, 5))
        else:
            need(("z", c, d, 2))
            put(("near", c, 1, d))

    def products(c, step):
        need(
            *(
                [],
                [("near", c, 0, 0), ("near", c, 0, 1)],
                [("z", c, 0, 0), ("z", c, 0, 1)],
                [("z", c, 1, 0), ("z", c, 1, 1)],
                [("z", c, 0, 2), ("z", c, 1, 2)],
                [("z", c, 0, 3), ("z", c, 0, 4)],
                [("z", c, 1, 3), ("z", c, 1, 4)],
                [("z", c, 0, 5), ("z", c, 1, 5)] if FAR_BY_Z[c] else [("near", c, 1, 0), ("near", c, 1, 1)],
            )[step]
        )
        g = c * STEPS + step
        u = order[step]
        fetch(g).wait()
        if PACKED[c]:
            k = NARROW.index(c)
            both = x_pack[k, u]
            turned = turn(both)
            columns = [beside(both, turned), beside(turned, both)]
            columns = columns if k == 0 else columns[::-1]
        else:
            columns = [x_wide[u, v] for v in range(2)]
        for v in range(2):
            high, low = split(columns[v])
            w[v, :, :HALF] = high
            w[v, :, HALF:] = low
        held = c % CHAINS

        def one(v, carry):
            for a in range(2):
                before = meta[0, a * 16 + u * 2 + v]
                for tile in range(2):
                    tall = slice(tile * 256, tile * 256 + 256)
                    b_high, b_low = split(blocks[g % BUFS, a, v, tall, :])
                    term = times(b_high, b_low, w[v], w[v, :, :HALF])
                    chain[held, step * 4 + v * 2 + a, tall, :] = term + chain[held, before, tall, :]
            return carry

        lax.fori_loop(0, 2, one, 0)
        if g + BUFS < PARTS * STEPS:
            fetch(g + BUFS).start()

    def total(c, i, its_core):
        dxh, dy = PAIRS[i] if PACKED[c] else UNITS[i][:2]
        first = ((xh + dxh) % 2) * 16 + ((y + dy) % 4) * 4 + its_core * 2
        if not PACKED[c]:
            return chain[c % CHAINS, meta[0, 32 + first + UNITS[i][2]]]
        pair = [chain[c % CHAINS, meta[0, 32 + first + e]] for e in range(2)]
        return beside(*(pair if NARROW.index(c) == 0 else pair[::-1]))

    def share_core(c, i):
        for before in range(c):
            if ("core", before, i) in started:
                started.pop(("core", before, i)).wait_send()
        give[i] = total(c, i, 1 - core)
        put(("core", c, i))

    def sum_core(c, i):
        need(("core", c, i))
        mine = total(c, i, core)
        if PACKED[c]:
            k = NARROW.index(c)
            s_pack[k, i] = s_pack[k, i] + mine
            units = [k for k in range(16) if UNITS[k][:2] == PAIRS[i]]
        else:
            s_wide[i] = s_wide[i] + mine
            units = [i]
        for unit in units:
            for d in range(2):
                if unit in Y_SEND[d][:4]:
                    put(("y", c, d, Y_SEND[d].index(unit)))
            if unit in X_SEND:
                put(("x", c, X_SEND.index(unit)))

    def y_add(c, i, js):
        for d in range(2):
            for j in js:
                if Y_ADD[d][j] == i:
                    add(c, i, False, "y", d, j)

    def pass_y(c, d, j):
        add(c, Y_ADD[d][j], False, "y", d, j)
        put(("y", c, d, 4 + j))

    def x_add(c, m):
        i = X_SEND[m] + 2
        add(c, i, True, "x", m)
        for d in range(2):
            if i in XY_SEND[d][:2]:
                put(("xy", c, d, XY_SEND[d].index(i)))

    def pass_xy(c, d):
        add(c, XY_ADD[d][0], True, "xy", d, 0)
        put(("xy", c, d, 2))

    def y_last(c, e):
        y_add(c, 12 + e, (2, 4))
        put(("last", c, e))

    def split_inv():
        fetch_rhs.wait()
        fetch_inv.wait()

        def one(i, carry):
            e, tall = i // 4, pl.ds(pl.multiple_of((i % 4) * 128, 128), 128)
            high, low = split(inv[e, tall, :])
            inv_high[e, tall, :] = high
            inv_low[e, tall, :] = low
            return carry

        lax.fori_loop(0, 8, one, 0)

    def finish(c, e):
        i = 14 + e
        y_add(c, i, (3, 5))
        for d in range(2):
            for j in (1, 2):
                if XY_ADD[d][j] == i:
                    add(c, i, True, "xy", d, j)
        add(c, i, False, "last", e)

    def top(wide, e):
        if wide:
            cols, update = slice(HALF, 2 * HALF), s_wide[14 + e]
        else:
            cols, pair = slice(0, HALF), PAIRS.index((0, 0))
            update = beside(*((s_pack[0, pair], s_pack[1, pair]) if e == 0 else (turn(s_pack[0, pair]), turn(s_pack[1, pair]))))
        high, low = split(rhs[e, :, cols] - update)
        both = jnp.concatenate([high, low], axis=1)
        top_out[e, :256, cols] = times(inv_high[e, :256, :256], inv_low[e, :256, :256], both[:256], high[:256])
        top_out[e, 256:, cols] = times(inv_high[e, 256:], inv_low[e, 256:], both, high)
        out(top_out.at[e, :, cols], top_to.at[e, :, cols], 2 + wide * 2 + e)

    tasks = {
        "leaf": leaf, "own": own, "zpass": zpass, "near": near, "far": far, "p": products, "inv": split_inv,
        "give": share_core, "sum": sum_core, "ypass": pass_y, "xadd": x_add, "xypass": pass_xy,
        "ylast": y_last, "fin": finish, "top": top, "chains": chains,
    }
    for name, *numbers in ORDER:
        tasks[name](*numbers)
    for copy in started.values():
        copy.wait_send()
    for copy in outs:
        copy.wait()


def hand_over(leaf_in, top_in, leaf_out, top_out, leaf, top, sem):
    pieces = [(ref.at[0, v], held.at[0, v], out.at[0, v]) for ref, held, out in ((leaf_in, leaf, leaf_out),) for v in range(2)]
    pieces += [
        (top_in.at[e, half], top.at[e, half], top_out.at[e, half])
        for e in range(2)
        for half in (pl.ds(0, 256), pl.ds(256, 256))
    ]
    loads = [pltpu.make_async_copy(src, held, sem.at[0, i]) for i, (src, held, _) in enumerate(pieces)]
    stores = [pltpu.make_async_copy(held, out, sem.at[1, i]) for i, (_, held, out) in enumerate(pieces)]
    for load in loads:
        load.start()
    for load, store in zip(loads, stores):
        load.wait()
        store.start()
    for store in stores:
        store.wait()


def per_device(leaf_rhs, leaf_inverse, off_blocks, ancestor_rows, block_present, top_rhs, top_inverse):
    wanted = jnp.where(block_present != 0, ancestor_rows, -1).reshape(-1)
    smem = pl.BlockSpec(memory_space=pltpu.SMEM)
    anywhere = pl.BlockSpec(memory_space=pl.ANY)
    dma = pltpu.SemaphoreType.DMA
    leaf, top = pl.pallas_call(
        kernel,
        out_shape=(
            jax.ShapeDtypeStruct(leaf_rhs.shape, F32),
            jax.ShapeDtypeStruct(top_rhs.shape, F32),
        ),
        in_specs=[smem] + [anywhere] * 5,
        out_specs=(anywhere, anywhere),
        scratch_shapes=[
            pltpu.VMEM(leaf_rhs.shape, F32),
            pltpu.VMEM(leaf_inverse.shape, F32),
            pltpu.VMEM(leaf_rhs.shape, F32),
            pltpu.VMEM(top_rhs.shape, F32),
            pltpu.VMEM((8, HALF), jnp.int32),
            pltpu.SMEM((8, HALF), jnp.int32),
            pltpu.VMEM((8, 2, W1, HALF), F32),
            pltpu.VMEM((2, 8, W1, HALF), F32),
            pltpu.VMEM((2, W1, 2 * HALF), BF16),
            pltpu.VMEM((BUFS, 2, 2, W2, W1), F32),
            pltpu.VMEM((CHAINS, NONE + 1, W2, HALF), F32),
            pltpu.VMEM((16, W2, HALF), F32),
            pltpu.VMEM((16, W2, HALF), F32),
            pltpu.VMEM((2, 8, W2, HALF), F32),
            pltpu.VMEM((2, 6, CUT, HALF), F32),
            pltpu.VMEM((2, 2, 6, CUT // 2, HALF), F32),
            pltpu.VMEM((2, 3, REST, HALF), F32),
            pltpu.VMEM((2, 2, 3, REST // 2, HALF), F32),
            pltpu.VMEM((8, REST, HALF), F32),
            pltpu.VMEM((2, 8, REST // 2, HALF), F32),
            pltpu.VMEM((2, CUT, HALF), F32),
            pltpu.VMEM((2, 2, CUT // 2, HALF), F32),
            pltpu.VMEM((2, W2, 2 * HALF), F32),
            pltpu.VMEM((2, W2, W2), F32),
            pltpu.VMEM((2, W2, W2), BF16),
            pltpu.VMEM((2, W2, W2), BF16),
            dma((BUFS,)),
            dma((2,)),
            dma((2,)),
            dma((6,)),
            dma((1,)),
            *(dma((PARTS, *shape)) for shape in ((2, 6), (2, 2), (16,), (2, 6), (2, 3), (8,), (2,)) for _ in range(2)),
        ],
        compiler_params=pltpu.CompilerParams(
            collective_id=0, has_side_effects=True, vmem_limit_bytes=60 * 1024 * 1024
        ),
        cost_estimate=pl.CostEstimate(flops=7_500_000_000, bytes_accessed=40_000_000, transcendentals=0),
    )(wanted, leaf_rhs, leaf_inverse, off_blocks, top_rhs, top_inverse)
    return pl.pallas_call(
        hand_over,
        out_shape=(jax.ShapeDtypeStruct(leaf_rhs.shape, F32), jax.ShapeDtypeStruct(top_rhs.shape, F32)),
        in_specs=[anywhere, anywhere],
        out_specs=(anywhere, anywhere),
        scratch_shapes=[pltpu.VMEM(leaf_rhs.shape, F32), pltpu.VMEM(top_rhs.shape, F32), dma((2, 6))],
    )(leaf, top)


def solution(mesh):
    return jax.shard_map(
        per_device,
        mesh=mesh,
        in_specs=(
            P("prow", "pcol", None, None),
            P("prow", "pcol", None, None),
            P("prow", None, None, "pcol", None, None),
            P("prow", None, None, "pcol"),
            P("prow", None, None, "pcol"),
            P(("prow", "pcol"), None, None),
            P(("prow", "pcol"), None, None),
        ),
        out_specs=(P("prow", "pcol", None, None), P(("prow", "pcol"), None, None)),
        check_vma=False,
    )
```

time: 95.2 us -> 89.5 us (0.940)
  Pallas kernels: 92 us -> 86.6 us
    pallas_call x1, Pallas kernels: 89.8 us -> 84.5 us  [per_device(): pl.pallas_call(kernel, out_shape=(jax.ShapeDtypeStruct(leaf_rhs.shape, F3...]
where the time goes in v3:
time: 89.5 us; the launch traced here: 88.8 us
  Pallas kernels  86.6 us (97%)
    pallas_call x1, Pallas kernels, per_device(): pl.pallas_call(kernel, out_shape=(jax.ShapeDtypeStruct(leaf_rhs.shape, F3...  84.5 us
    pallas_call x1, Pallas kernels, per_device(): pl.pallas_call(hand_over, out_shape=(jax.ShapeDtypeStruct(leaf_rhs.shape,...  2.19 us

profile of v3, /device:TPU:1, one launch (start us, length us, event | category | flops | bytes accessed | tf_op | source)
XLA Modules:
  0.0 88.8 jit_solution(8384544698059530841)
XLA Ops:
  0.6 0.7 compare_select_fusion
  1.3 0.1 copy.10
  1.4 0.6 reshape.7.wanted
  2.0 84.5 %shard_map.86 = (f32[1,2,256,256]{3,2,1,0:T(8,128)}, f32[2,512,256]{2,1,0:T(8,128)}) custom-call(s32[32]{0:T(128)} %reshape.7.wanted, f32[1,2,256,256]{3,2,1,0:T(8,128)} %leaf_rhs_in.1, f32[1,2,256,256]{3,2,1,0:T(8,128)} %leaf_inv_in.1, f32[1,2,8,2,512,256]{5,4,3,2,1,0:T(8,128)} %off_blocks.1, f32[2,512,256]{2,1,0:T(8,128)} %top_rhs.1, f32[2,512,512]{2,1,0:T(8,128)} %top_inv.1), custom_call_target="tpu_custom_call" | custom-call | flops 7500000256 | bytes 40000000 | tf_op jit(solution)/shard_map/pallas_call | solution.py:441
  86.5 2.2 %shard_map.87 = (f32[1,2,256,256]{3,2,1,0:T(8,128)}, f32[2,512,256]{2,1,0:T(8,128)}) custom-call(f32[1,2,256,256]{3,2,1,0:T(8,128)} %get-tuple-element.4.leaf_in, f32[2,512,256]{2,1,0:T(8,128)} %get-tuple-element.5.top_in), custom_call_target="tpu_custom_call" | custom-call | tf_op jit(solution)/shard_map/pallas_call | solution.py:488

commit v4 on v3

--- a/solution.py
+++ b/solution.py
@@ -10,14 +10,15 @@
 W1, W2, HALF = 256, 512, 128
 STEPS = 8
 BUFS = 3
-CUT = 320
-REST = W2 - CUT
+CUT, REST = 296, 216
+CUT_PACKED, REST_PACKED = 144, 112
 NONE = 32
 PACKED = (True, True, False)
 PARTS = len(PACKED)
 NARROW = tuple(c for c in range(PARTS) if PACKED[c])
 CHAINS = 2
-FAR_BY_Z = (False, True, True)
+X_ONLY, BOTH, Z_ONLY = 0, 2, 1
+FAR_BY = (2, 1, 1)
 
 UNITS = (
     (1, 2, 0), (1, 2, 1), (0, 2, 0), (0, 2, 1),
@@ -34,32 +35,34 @@
 
 
 ORDER = (
-    ("leaf", 0), ("own", 0), ("chains",), ("leaf", 2), ("p", 0, 0), ("inv",), ("zpass", 0, 0), ("zpass", 0, 1),
-    ("near", 0, 0), ("near", 0, 1), ("p", 0, 1), ("p", 0, 2), ("far", 0, 0), ("far", 0, 1), ("own", 1), ("p", 0, 3),
-    ("p", 0, 4), ("p", 0, 5), ("p", 0, 6), ("zpass", 1, 1), ("zpass", 1, 0), ("p", 0, 7), ("give", 0, 0),
-    ("give", 0, 1), ("give", 0, 2), ("near", 1, 0), ("give", 0, 3), ("give", 0, 4), ("p", 1, 0), ("near", 1, 1),
-    ("p", 1, 1), ("sum", 0, 0), ("p", 1, 2), ("far", 1, 0), ("sum", 0, 1), ("p", 1, 3), ("far", 1, 1), ("own", 2),
-    ("sum", 0, 2), ("sum", 0, 3), ("sum", 0, 4), ("give", 0, 5), ("give", 0, 6), ("give", 0, 7), ("xadd", 0, 0),
-    ("p", 1, 4), ("p", 1, 5), ("ypass", 0, 0, 1), ("xadd", 0, 1), ("ypass", 0, 0, 0), ("sum", 0, 5),
-    ("ypass", 0, 1, 1), ("p", 1, 6), ("p", 1, 7), ("give", 1, 0), ("sum", 0, 6), ("sum", 0, 7), ("near", 2, 0),
-    ("p", 2, 0), ("give", 1, 1), ("give", 1, 2), ("zpass", 2, 0), ("ypass", 0, 1, 0), ("p", 2, 1), ("xadd", 0, 2),
-    ("near", 2, 1), ("sum", 1, 0), ("give", 1, 3), ("zpass", 2, 1), ("p", 2, 2), ("sum", 1, 1), ("p", 2, 3),
-    ("xadd", 0, 3), ("xadd", 0, 4), ("xypass", 0, 0), ("far", 2, 0), ("ylast", 0, 1), ("xadd", 0, 5),
-    ("xypass", 0, 1), ("ylast", 0, 0), ("sum", 1, 2), ("sum", 1, 3), ("give", 1, 4), ("give", 1, 5), ("give", 1, 6),
-    ("give", 1, 7), ("xadd", 0, 6), ("ypass", 1, 1, 0), ("ypass", 1, 0, 0), ("xadd", 0, 7), ("far", 2, 1),
-    ("xadd", 1, 0), ("sum", 1, 4), ("ypass", 1, 0, 1), ("sum", 1, 5), ("xadd", 1, 1), ("ypass", 1, 1, 1),
-    ("sum", 1, 6), ("sum", 1, 7), ("p", 2, 4), ("p", 2, 5), ("p", 2, 6), ("p", 2, 7), ("give", 2, 0),
-    ("ylast", 1, 1), ("xadd", 1, 2), ("xadd", 1, 4), ("xypass", 1, 0), ("give", 2, 1), ("give", 2, 2),
-    ("give", 2, 3), ("give", 2, 4), ("give", 2, 5), ("fin", 0, 0), ("xadd", 1, 3), ("give", 2, 6), ("give", 2, 7),
-    ("give", 2, 8), ("give", 2, 9), ("give", 2, 10), ("give", 2, 11), ("give", 2, 12), ("give", 2, 13),
-    ("give", 2, 14), ("give", 2, 15), ("xadd", 1, 5), ("xypass", 1, 1), ("ylast", 1, 0), ("sum", 2, 0),
-    ("fin", 0, 1), ("xadd", 1, 6), ("sum", 2, 1), ("sum", 2, 2), ("sum", 2, 3), ("xadd", 1, 7), ("sum", 2, 4),
-    ("sum", 2, 5), ("sum", 2, 6), ("fin", 1, 1), ("sum", 2, 7), ("sum", 2, 8), ("sum", 2, 9), ("fin", 1, 0),
-    ("sum", 2, 10), ("top", 0, 1), ("ypass", 2, 0, 0), ("sum", 2, 11), ("sum", 2, 12), ("top", 0, 0),
-    ("ypass", 2, 1, 0), ("sum", 2, 13), ("sum", 2, 14), ("xadd", 2, 0), ("sum", 2, 15), ("xadd", 2, 1),
+    ("leaf", 0), ("ownx", 0, 1), ("ownz", 0), ("ownx", 0, 0), ("chains",), ("p", 0, 0), ("leaf", 2), ("ownx", 1, 1),
+    ("ownx", 1, 0), ("inv",), ("near", 0, 1), ("zpass", 0, 0), ("zpass", 0, 1), ("near", 0, 0), ("p", 0, 1),
+    ("p", 0, 2), ("p", 0, 3), ("far", 0, 1), ("far", 0, 0), ("ownz", 1), ("near", 1, 1), ("p", 0, 4), ("near", 1, 0),
+    ("ownx", 2, 1), ("ownx", 2, 0), ("p", 0, 5), ("p", 0, 6), ("p", 0, 7), ("give", 0, 0), ("zpass", 1, 0),
+    ("give", 0, 1), ("p", 1, 0), ("p", 1, 1), ("give", 0, 2), ("zpass", 1, 1), ("give", 0, 3), ("give", 0, 4),
+    ("give", 0, 5), ("far", 1, 1), ("sum", 0, 0), ("give", 0, 6), ("give", 0, 7), ("p", 1, 2), ("far", 1, 0),
+    ("sum", 0, 1), ("ownz", 2), ("near", 2, 1), ("p", 1, 3), ("near", 2, 0), ("sum", 0, 2), ("sum", 0, 3),
+    ("p", 1, 4), ("sum", 0, 4), ("ypass", 0, 1, 0), ("sum", 0, 5), ("xadd", 0, 0), ("sum", 0, 6), ("xadd", 0, 1),
+    ("sum", 0, 7), ("ypass", 0, 0, 0), ("p", 1, 5), ("ypass", 0, 1, 1), ("ypass", 0, 0, 1), ("p", 1, 6),
+    ("zpass", 2, 1), ("xadd", 0, 2), ("p", 1, 7), ("give", 1, 0), ("give", 1, 1), ("give", 1, 2), ("ylast", 0, 1),
+    ("xadd", 0, 3), ("xadd", 0, 4), ("zpass", 2, 0), ("p", 2, 0), ("xadd", 0, 5), ("give", 1, 3), ("give", 1, 4),
+    ("give", 1, 5), ("give", 1, 6), ("give", 1, 7), ("p", 2, 1), ("sum", 1, 0), ("xypass", 0, 1), ("sum", 1, 1),
+    ("xadd", 0, 6), ("sum", 1, 2), ("ylast", 0, 0), ("xadd", 0, 7), ("xypass", 0, 0), ("p", 2, 2), ("far", 2, 1),
+    ("p", 2, 3), ("finy", 0, 1), ("sum", 1, 3), ("sum", 1, 4), ("sum", 1, 5), ("sum", 1, 6), ("sum", 1, 7),
+    ("xadd", 1, 0), ("ypass", 1, 1, 0), ("ypass", 1, 0, 0), ("far", 2, 0), ("xadd", 1, 1), ("finx", 0, 1),
+    ("ypass", 1, 0, 1), ("xadd", 1, 2), ("ypass", 1, 1, 1), ("p", 2, 4), ("p", 2, 5), ("xadd", 1, 4), ("finx", 0, 0),
+    ("p", 2, 6), ("p", 2, 7), ("xypass", 1, 0), ("give", 2, 0), ("xadd", 1, 3), ("xadd", 1, 5), ("ylast", 1, 1),
+    ("finy", 0, 0), ("give", 2, 1), ("give", 2, 2), ("give", 2, 3), ("give", 2, 4), ("give", 2, 5), ("xadd", 1, 6),
+    ("give", 2, 6), ("give", 2, 7), ("ylast", 1, 0), ("xypass", 1, 1), ("give", 2, 8), ("give", 2, 9),
+    ("give", 2, 10), ("give", 2, 11), ("give", 2, 12), ("give", 2, 13), ("xadd", 1, 7), ("give", 2, 14),
+    ("give", 2, 15), ("sum", 2, 0), ("sum", 2, 1), ("sum", 2, 2), ("finy", 1, 1), ("sum", 2, 3), ("sum", 2, 4),
+    ("sum", 2, 5), ("finx", 1, 1), ("finx", 1, 0), ("finy", 1, 0), ("top", 1), ("top", 0), ("sum", 2, 6),
+    ("sum", 2, 7), ("sum", 2, 8), ("sum", 2, 9), ("xadd", 2, 0), ("sum", 2, 10), ("sum", 2, 11), ("ypass", 2, 0, 0),
+    ("ypass", 2, 1, 0), ("sum", 2, 12), ("sum", 2, 13), ("sum", 2, 14), ("xadd", 2, 1), ("sum", 2, 15),
     ("ypass", 2, 0, 1), ("ypass", 2, 1, 1), ("xadd", 2, 2), ("xadd", 2, 3), ("xadd", 2, 4), ("xadd", 2, 5),
-    ("xadd", 2, 6), ("ylast", 2, 0), ("ylast", 2, 1), ("xadd", 2, 7), ("xypass", 2, 0), ("xypass", 2, 1),
-    ("fin", 2, 0), ("top", 1, 0), ("fin", 2, 1), ("top", 1, 1),
+    ("xypass", 2, 0), ("ylast", 2, 1), ("xadd", 2, 6), ("ylast", 2, 0), ("xypass", 2, 1), ("xadd", 2, 7),
+    ("finy", 2, 1), ("topa", 1), ("finy", 2, 0), ("topa", 0), ("finx", 2, 0), ("topb", 0), ("finx", 2, 1),
+    ("topb", 1),
 )
 
 def split(value):
@@ -77,8 +80,8 @@
 
 
 def kernel(
-    wanted, leaf_rhs_in, leaf_inv_in, off_blocks, top_rhs, top_inv, leaf_to, top_to,
-    leaf_rhs, leaf_inv, leaf_out, top_out, found, meta,
+    wanted_in, leaf_rhs_in, leaf_inv_in, off_blocks, top_rhs, top_inv, leaf_to, top_to,
+    leaf_rhs, leaf_inv, leaf_out, top_out, wanted, found, meta,
     x_wide, x_pack, w, blocks, chain, give, s_wide, s_pack, y_wide, y_pack, xy_wide, xy_pack, far_wide, far_pack,
     last_wide, last_pack, rhs, inv, inv_high, inv_low,
     block_sem, top_sem, leaf_sem, out_sem, meta_sem, az_s, az_r, ax_s, ax_r, core_s, core_r, y_s, y_r, xy_s, xy_r, x_s, x_r, x2_s, x2_r,
@@ -126,7 +129,7 @@
         if not PACKED[c]:
             return s_wide, (i, pl.ds(CUT, REST) if high else pl.ds(0, CUT))
         pair, k = PAIRS.index(UNITS[i][:2]), UNITS[i][2]
-        rows = pl.ds(CUT + k * (REST // 2), REST // 2) if high else pl.ds(k * (CUT // 2), CUT // 2)
+        rows = pl.ds(2 * CUT_PACKED + k * REST_PACKED, REST_PACKED) if high else pl.ds(k * CUT_PACKED, CUT_PACKED)
         return s_pack, (NARROW.index(c), pair, rows)
 
     def arrived(c, kind, *index):
@@ -143,7 +146,8 @@
         pltpu.make_async_copy(src, dst, leaf_sem.at[i])
         for i, (src, dst) in enumerate(((leaf_inv_in, leaf_inv), (leaf_rhs_in, leaf_rhs)))
     ]
-    for copy in fetch_leaf:
+    fetch_wanted = pltpu.make_async_copy(wanted_in, wanted, meta_sem.at[1])
+    for copy in (*fetch_leaf, fetch_wanted):
         copy.start()
 
     barrier = pltpu.get_barrier_semaphore()
@@ -167,6 +171,8 @@
     started, seen = {}, set()
 
     def put(key):
+        if not started:
+            pl.semaphore_wait(barrier, len(partners))
         started[key] = message(*key)
         started[key].start()
 
@@ -225,6 +231,7 @@
                 out(leaf_out.at[0, v], leaf_to.at[0, v], v)
 
     def chains():
+        fetch_wanted.wait()
         lane = lax.broadcasted_iota(jnp.int32, (8, HALF), 1)
         ask, limit, slots = lane - 32, jnp.full((8, HALF), 32, jnp.int32), []
         for step in range(STEPS):
@@ -242,11 +249,11 @@
         copy.start()
         copy.wait()
 
-    def own(c):
-        if c == 0:
-            pl.semaphore_wait(barrier, len(partners))
+    def own_x(c, v):
+        put(("near", c, 0, v))
+
+    def own_z(c):
         for j in range(2):
-            put(("near", c, 0, j))
             for d in range(2):
                 put(("z", c, d, j))
 
@@ -260,7 +267,7 @@
             put(("z", c, d, 3 + j))
 
     def far(c, d):
-        if FAR_BY_Z[c]:
+        if FAR_BY[c] == Z_ONLY or (FAR_BY[c] == BOTH and d == 1):
             need(("z", c, d, 3 + d))
             put(("z", c, d, 5))
         else:
@@ -277,7 +284,10 @@
                 [("z", c, 0, 2), ("z", c, 1, 2)],
                 [("z", c, 0, 3), ("z", c, 0, 4)],
                 [("z", c, 1, 3), ("z", c, 1, 4)],
-                [("z", c, 0, 5), ("z", c, 1, 5)] if FAR_BY_Z[c] else [("near", c, 1, 0), ("near", c, 1, 1)],
+                [
+                    ("near", c, 1, d) if FAR_BY[c] == X_ONLY or (FAR_BY[c] == BOTH and d == 0) else ("z", c, d, 5)
+                    for d in range(2)
+                ],
             )[step]
         )
         g = c * STEPS + step
@@ -297,7 +307,7 @@
             w[v, :, HALF:] = low
         held = c % CHAINS
 
-        def one(v, carry):
+        def one(v, carry=0):
             for a in range(2):
                 before = meta[0, a * 16 + u * 2 + v]
                 for tile in range(2):
@@ -307,7 +317,10 @@
                     chain[held, step * 4 + v * 2 + a, tall, :] = term + chain[held, before, tall, :]
             return carry
 
-        lax.fori_loop(0, 2, one, 0)
+        if c == 0:
+            one(0), one(1)
+        else:
+            lax.fori_loop(0, 2, one, 0)
         if g + BUFS < PARTS * STEPS:
             fetch(g + BUFS).start()
 
@@ -381,31 +394,48 @@
 
         lax.fori_loop(0, 8, one, 0)
 
-    def finish(c, e):
-        i = 14 + e
-        y_add(c, i, (3, 5))
+    def finish_y(c, e):
+        y_add(c, 14 + e, (3, 5))
+        add(c, 14 + e, False, "last", e)
+
+    def finish_xy(c, e):
         for d in range(2):
             for j in (1, 2):
-                if XY_ADD[d][j] == i:
-                    add(c, i, True, "xy", d, j)
-        add(c, i, False, "last", e)
-
-    def top(wide, e):
-        if wide:
-            cols, update = slice(HALF, 2 * HALF), s_wide[14 + e]
-        else:
-            cols, pair = slice(0, HALF), PAIRS.index((0, 0))
-            update = beside(*((s_pack[0, pair], s_pack[1, pair]) if e == 0 else (turn(s_pack[0, pair]), turn(s_pack[1, pair]))))
-        high, low = split(rhs[e, :, cols] - update)
+                if XY_ADD[d][j] == 14 + e:
+                    add(c, 14 + e, True, "xy", d, j)
+
+    def block_times(e, below, right, value):
+        high, low = split(value)
         both = jnp.concatenate([high, low], axis=1)
-        top_out[e, :256, cols] = times(inv_high[e, :256, :256], inv_low[e, :256, :256], both[:256], high[:256])
-        top_out[e, 256:, cols] = times(inv_high[e, 256:], inv_low[e, 256:], both, high)
-        out(top_out.at[e, :, cols], top_to.at[e, :, cols], 2 + wide * 2 + e)
+        return times(inv_high[e, below, right], inv_low[e, below, right], both, high)
+
+    upper, lower, whole = slice(0, 256), slice(256, W2), slice(0, W2)
+    narrow_cols, wide_cols = slice(0, HALF), slice(HALF, 2 * HALF)
+
+    def top(e):
+        pair = PAIRS.index((0, 0))
+        sums = [s_pack[k, pair] for k in range(2)]
+        value = rhs[e, :, narrow_cols] - (beside(*sums) if e == 0 else beside(*map(turn, sums)))
+        top_out[e, upper, narrow_cols] = block_times(e, upper, upper, value[:256])
+        top_out[e, lower, narrow_cols] = block_times(e, lower, whole, value)
+        out(top_out.at[e, :, narrow_cols], top_to.at[e, :, narrow_cols], 2 + e)
+
+    def top_upper(e):
+        value = rhs[e, upper, wide_cols] - s_wide[14 + e, upper]
+        top_out[e, upper, wide_cols] = block_times(e, upper, upper, value)
+        top_out[e, lower, wide_cols] = block_times(e, lower, upper, value)
+        out(top_out.at[e, upper, wide_cols], top_to.at[e, upper, wide_cols], 4 + e)
+
+    def top_lower(e):
+        value = rhs[e, lower, wide_cols] - s_wide[14 + e, lower]
+        top_out[e, lower, wide_cols] = top_out[e, lower, wide_cols] + block_times(e, lower, lower, value)
+        out(top_out.at[e, lower, wide_cols], top_to.at[e, lower, wide_cols], 6 + e)
 
     tasks = {
-        "leaf": leaf, "own": own, "zpass": zpass, "near": near, "far": far, "p": products, "inv": split_inv,
+        "leaf": leaf, "ownx": own_x, "ownz": own_z, "zpass": zpass, "near": near, "far": far, "p": products, "inv": split_inv,
         "give": share_core, "sum": sum_core, "ypass": pass_y, "xadd": x_add, "xypass": pass_xy,
-        "ylast": y_last, "fin": finish, "top": top, "chains": chains,
+        "ylast": y_last, "finy": finish_y, "finx": finish_xy, "top": top, "topa": top_upper, "topb": top_lower,
+        "chains": chains,
     }
     for name, *numbers in ORDER:
         tasks[name](*numbers)
@@ -435,7 +465,6 @@
 
 def per_device(leaf_rhs, leaf_inverse, off_blocks, ancestor_rows, block_present, top_rhs, top_inverse):
     wanted = jnp.where(block_present != 0, ancestor_rows, -1).reshape(-1)
-    smem = pl.BlockSpec(memory_space=pltpu.SMEM)
     anywhere = pl.BlockSpec(memory_space=pl.ANY)
     dma = pltpu.SemaphoreType.DMA
     leaf, top = pl.pallas_call(
@@ -444,13 +473,14 @@
             jax.ShapeDtypeStruct(leaf_rhs.shape, F32),
             jax.ShapeDtypeStruct(top_rhs.shape, F32),
         ),
-        in_specs=[smem] + [anywhere] * 5,
+        in_specs=[anywhere] * 6,
         out_specs=(anywhere, anywhere),
         scratch_shapes=[
             pltpu.VMEM(leaf_rhs.shape, F32),
             pltpu.VMEM(leaf_inverse.shape, F32),
             pltpu.VMEM(leaf_rhs.shape, F32),
             pltpu.VMEM(top_rhs.shape, F32),
+            pltpu.SMEM((32,), jnp.int32),
             pltpu.VMEM((8, HALF), jnp.int32),
             pltpu.SMEM((8, HALF), jnp.int32),
             pltpu.VMEM((8, 2, W1, HALF), F32),
@@ -462,13 +492,13 @@
             pltpu.VMEM((16, W2, HALF), F32),
             pltpu.VMEM((2, 8, W2, HALF), F32),
             pltpu.VMEM((2, 6, CUT, HALF), F32),
-            pltpu.VMEM((2, 2, 6, CUT // 2, HALF), F32),
+            pltpu.VMEM((2, 2, 6, CUT_PACKED, HALF), F32),
             pltpu.VMEM((2, 3, REST, HALF), F32),
-            pltpu.VMEM((2, 2, 3, REST // 2, HALF), F32),
+            pltpu.VMEM((2, 2, 3, REST_PACKED, HALF), F32),
             pltpu.VMEM((8, REST, HALF), F32),
-            pltpu.VMEM((2, 8, REST // 2, HALF), F32),
+            pltpu.VMEM((2, 8, REST_PACKED, HALF), F32),
             pltpu.VMEM((2, CUT, HALF), F32),
-            pltpu.VMEM((2, 2, CUT // 2, HALF), F32),
+            pltpu.VMEM((2, 2, CUT_PACKED, HALF), F32),
             pltpu.VMEM((2, W2, 2 * HALF), F32),
             pltpu.VMEM((2, W2, W2), F32),
             pltpu.VMEM((2, W2, W2), BF16),
@@ -476,8 +506,8 @@
             dma((BUFS,)),
             dma((2,)),
             dma((2,)),
-            dma((6,)),
-            dma((1,)),
+            dma((8,)),
+            dma((2,)),
             *(dma((PARTS, *shape)) for shape in ((2, 6), (2, 2), (16,), (2, 6), (2, 3), (8,), (2,)) for _ in range(2)),
         ],
         compiler_params=pltpu.CompilerParams(

time: 89.5 us -> 86.4 us (0.965)
  Pallas kernels: 86.6 us -> 83.9 us
    pallas_call x1, Pallas kernels: 84.5 us -> 81.7 us  [per_device(): pl.pallas_call(kernel, out_shape=(jax.ShapeDtypeStruct(leaf_rhs.shape, F3...]
where the time goes in v4:
time: 86.4 us; the launch traced here: 86.1 us
  Pallas kernels  83.9 us (97%)
    pallas_call x1, Pallas kernels, per_device(): pl.pallas_call(kernel, out_shape=(jax.ShapeDtypeStruct(leaf_rhs.shape, F3...  81.7 us
    pallas_call x1, Pallas kernels, per_device(): pl.pallas_call(hand_over, out_shape=(jax.ShapeDtypeStruct(leaf_rhs.shape,...  2.19 us

profile of v4, /device:TPU:1, one launch (start us, length us, event | category | flops | bytes accessed | tf_op | source)
XLA Modules:
  0.0 86.1 jit_solution(4619675589660256950)
XLA Ops:
  0.6 0.7 compare_select_fusion
  1.3 0.1 copy.10
  1.4 0.6 reshape.7.wanted_in
  2.0 81.7 %shard_map.86 = (f32[1,2,256,256]{3,2,1,0:T(8,128)}, f32[2,512,256]{2,1,0:T(8,128)}) custom-call(s32[32]{0:T(128)} %reshape.7.wanted_in, f32[1,2,256,256]{3,2,1,0:T(8,128)} %leaf_rhs_in.1, f32[1,2,256,256]{3,2,1,0:T(8,128)} %leaf_inv_in.1, f32[1,2,8,2,512,256]{5,4,3,2,1,0:T(8,128)} %off_blocks.1, f32[2,512,256]{2,1,0:T(8,128)} %top_rhs.1, f32[2,512,512]{2,1,0:T(8,128)} %top_inv.1), custom_call_target="tpu_custom_call" | custom-call | flops 7500000256 | bytes 40000000 | tf_op jit(solution)/shard_map/pallas_call | solution.py:470
  83.8 2.2 %shard_map.87 = (f32[1,2,256,256]{3,2,1,0:T(8,128)}, f32[2,512,256]{2,1,0:T(8,128)}) custom-call(f32[1,2,256,256]{3,2,1,0:T(8,128)} %get-tuple-element.4.leaf_in, f32[2,512,256]{2,1,0:T(8,128)} %get-tuple-element.5.top_in), custom_call_target="tpu_custom_call" | custom-call | tf_op jit(solution)/shard_map/pallas_call | solution.py:518

commit v5 on v4

--- a/solution.py
+++ b/solution.py
@@ -80,11 +80,11 @@
 
 
 def kernel(
-    wanted_in, leaf_rhs_in, leaf_inv_in, off_blocks, top_rhs, top_inv, leaf_to, top_to,
-    leaf_rhs, leaf_inv, leaf_out, top_out, wanted, found, meta,
+    wanted_in, leaf_rhs_in, leaf_inv_in, off_blocks, top_rhs, top_inv, leaf_out, top_out,
+    leaf_rhs, leaf_inv, wanted, found, meta,
     x_wide, x_pack, w, blocks, chain, give, s_wide, s_pack, y_wide, y_pack, xy_wide, xy_pack, far_wide, far_pack,
     last_wide, last_pack, rhs, inv, inv_high, inv_low,
-    block_sem, top_sem, leaf_sem, out_sem, meta_sem, az_s, az_r, ax_s, ax_r, core_s, core_r, y_s, y_r, xy_s, xy_r, x_s, x_r, x2_s, x2_r,
+    block_sem, top_sem, leaf_sem, meta_sem, az_s, az_r, ax_s, ax_r, core_s, core_r, y_s, y_r, xy_s, xy_r, x_s, x_r, x2_s, x2_r,
 ):
     row, col = lax.axis_index("prow"), lax.axis_index("pcol")
     z, xl = row // 2, row % 2
@@ -205,12 +205,6 @@
         dst, at_dst = arrived(c, kind, *index)
         return send(src.at[at_src], dst.at[at_dst], sems[0].at[(c, *index)], sems[1].at[(c, *index)], device)
 
-    outs = []
-
-    def out(src, dst, i):
-        outs.append(pltpu.make_async_copy(src, dst, out_sem.at[i]))
-        outs[-1].start()
-
     def solve(v, cols):
         i_high, i_low = split(leaf_inv[0, v])
         r_high, r_low = split(leaf_rhs[0, v, :, cols])
@@ -227,8 +221,6 @@
         else:
             for v in range(2):
                 x_wide[row, v] = solve(v, slice(HALF, 2 * HALF))
-            for v in range(2):
-                out(leaf_out.at[0, v], leaf_to.at[0, v], v)
 
     def chains():
         fetch_wanted.wait()
@@ -418,18 +410,15 @@
         value = rhs[e, :, narrow_cols] - (beside(*sums) if e == 0 else beside(*map(turn, sums)))
         top_out[e, upper, narrow_cols] = block_times(e, upper, upper, value[:256])
         top_out[e, lower, narrow_cols] = block_times(e, lower, whole, value)
-        out(top_out.at[e, :, narrow_cols], top_to.at[e, :, narrow_cols], 2 + e)
 
     def top_upper(e):
         value = rhs[e, upper, wide_cols] - s_wide[14 + e, upper]
         top_out[e, upper, wide_cols] = block_times(e, upper, upper, value)
         top_out[e, lower, wide_cols] = block_times(e, lower, upper, value)
-        out(top_out.at[e, upper, wide_cols], top_to.at[e, upper, wide_cols], 4 + e)
 
     def top_lower(e):
         value = rhs[e, lower, wide_cols] - s_wide[14 + e, lower]
         top_out[e, lower, wide_cols] = top_out[e, lower, wide_cols] + block_times(e, lower, lower, value)
-        out(top_out.at[e, lower, wide_cols], top_to.at[e, lower, wide_cols], 6 + e)
 
     tasks = {
         "leaf": leaf, "ownx": own_x, "ownz": own_z, "zpass": zpass, "near": near, "far": far, "p": products, "inv": split_inv,
@@ -441,45 +430,31 @@
         tasks[name](*numbers)
     for copy in started.values():
         copy.wait_send()
-    for copy in outs:
+
+
+def hand_over(leaf_in, top_in, leaf_out, top_out, sem):
+    pieces = [(leaf_in.at[0, v], leaf_out.at[0, v]) for v in range(2)]
+    pieces += [(top_in.at[e, half], top_out.at[e, half]) for e in range(2) for half in (pl.ds(0, 256), pl.ds(256, 256))]
+    copies = [pltpu.make_async_copy(src, dst, sem.at[i]) for i, (src, dst) in enumerate(pieces)]
+    for copy in copies:
+        copy.start()
+    for copy in copies:
         copy.wait()
-
-
-def hand_over(leaf_in, top_in, leaf_out, top_out, leaf, top, sem):
-    pieces = [(ref.at[0, v], held.at[0, v], out.at[0, v]) for ref, held, out in ((leaf_in, leaf, leaf_out),) for v in range(2)]
-    pieces += [
-        (top_in.at[e, half], top.at[e, half], top_out.at[e, half])
-        for e in range(2)
-        for half in (pl.ds(0, 256), pl.ds(256, 256))
-    ]
-    loads = [pltpu.make_async_copy(src, held, sem.at[0, i]) for i, (src, held, _) in enumerate(pieces)]
-    stores = [pltpu.make_async_copy(held, out, sem.at[1, i]) for i, (_, held, out) in enumerate(pieces)]
-    for load in loads:
-        load.start()
-    for load, store in zip(loads, stores):
-        load.wait()
-        store.start()
-    for store in stores:
-        store.wait()
 
 
 def per_device(leaf_rhs, leaf_inverse, off_blocks, ancestor_rows, block_present, top_rhs, top_inverse):
     wanted = jnp.where(block_present != 0, ancestor_rows, -1).reshape(-1)
     anywhere = pl.BlockSpec(memory_space=pl.ANY)
+    vmem = pl.BlockSpec(memory_space=pltpu.VMEM)
     dma = pltpu.SemaphoreType.DMA
     leaf, top = pl.pallas_call(
         kernel,
-        out_shape=(
-            jax.ShapeDtypeStruct(leaf_rhs.shape, F32),
-            jax.ShapeDtypeStruct(top_rhs.shape, F32),
-        ),
-        in_specs=[anywhere] * 6,
-        out_specs=(anywhere, anywhere),
+        out_shape=(pltpu.VMEM(leaf_rhs.shape, F32), pltpu.VMEM(top_rhs.shape, F32)),
+        in_specs=[vmem] + [anywhere] * 5,
+        out_specs=(vmem, vmem),
         scratch_shapes=[
             pltpu.VMEM(leaf_rhs.shape, F32),
             pltpu.VMEM(leaf_inverse.shape, F32),
-            pltpu.VMEM(leaf_rhs.shape, F32),
-            pltpu.VMEM(top_rhs.shape, F32),
             pltpu.SMEM((32,), jnp.int32),
             pltpu.VMEM((8, HALF), jnp.int32),
             pltpu.SMEM((8, HALF), jnp.int32),
@@ -506,7 +481,6 @@
             dma((BUFS,)),
             dma((2,)),
             dma((2,)),
-            dma((8,)),
             dma((2,)),
             *(dma((PARTS, *shape)) for shape in ((2, 6), (2, 2), (16,), (2, 6), (2, 3), (8,), (2,)) for _ in range(2)),
         ],
@@ -514,14 +488,14 @@
             collective_id=0, has_side_effects=True, vmem_limit_bytes=60 * 1024 * 1024
         ),
         cost_estimate=pl.CostEstimate(flops=7_500_000_000, bytes_accessed=40_000_000, transcendentals=0),
-    )(wanted, leaf_rhs, leaf_inverse, off_blocks, top_rhs, top_inverse)
+    )(pltpu.with_memory_space_constraint(wanted, pltpu.VMEM), leaf_rhs, leaf_inverse, off_blocks, top_rhs, top_inverse)
     return pl.pallas_call(
         hand_over,
         out_shape=(jax.ShapeDtypeStruct(leaf_rhs.shape, F32), jax.ShapeDtypeStruct(top_rhs.shape, F32)),
-        in_specs=[anywhere, anywhere],
+        in_specs=[vmem, vmem],
         out_specs=(anywhere, anywhere),
-        scratch_shapes=[pltpu.VMEM(leaf_rhs.shape, F32), pltpu.VMEM(top_rhs.shape, F32), dma((2, 6))],
-    )(leaf, top)
+        scratch_shapes=[dma((6,))],
+    )(*(pltpu.with_memory_space_constraint(value, pltpu.VMEM) for value in (leaf, top)))
 
 
 def solution(mesh):

time: 86.4 us -> 84.5 us (0.978)
  Pallas kernels: 83.9 us -> 82.5 us
    pallas_call x1, Pallas kernels: 2.19 us -> 1.19 us  [per_device(): pl.pallas_call(hand_over, out_shape=(jax.ShapeDtypeStruct(leaf_rhs.shape,...]
where the time goes in v5:
time: 84.5 us; the launch traced here: 84.2 us
  Pallas kernels  82.5 us (98%)
    pallas_call x1, Pallas kernels, per_device(): pl.pallas_call(kernel, out_shape=(pltpu.VMEM(leaf_rhs.shape, F32), pltpu....  81.3 us

profile of v5, /device:TPU:1, one launch (start us, length us, event | category | flops | bytes accessed | tf_op | source)
XLA Modules:
  0.0 84.2 jit_solution(11177896513232369617)
XLA Ops:
  0.6 0.7 compare_select_fusion
  1.3 0.1 copy.10
  1.4 0.1 reshape.7.wanted_in
  1.5 81.3 %shard_map.86 = (f32[1,2,256,256]{3,2,1,0:T(8,128)S(1)}, f32[2,512,256]{2,1,0:T(8,128)S(1)}) custom-call(s32[32]{0:T(128)S(1)} %reshape.7.wanted_in, f32[1,2,256,256]{3,2,1,0:T(8,128)} %leaf_rhs_in.1, f32[1,2,256,256]{3,2,1,0:T(8,128)} %leaf_inv_in.1, f32[1,2,8,2,512,256]{5,4,3,2,1,0:T(8,128)} %off_blocks.1, f32[2,512,256]{2,1,0:T(8,128)} %top_rhs.1, ...), custom_call_target="tpu_custom_call" | custom-call | flops 7500000256 | bytes 40000000 | tf_op jit(solution)/shard_map/pallas_call | solution.py:450
  82.8 1.2 %shard_map.87 = (f32[1,2,256,256]{3,2,1,0:T(8,128)}, f32[2,512,256]{2,1,0:T(8,128)}) custom-call(f32[1,2,256,256]{3,2,1,0:T(8,128)S(1)} %get-tuple-element.4.leaf_in, f32[2,512,256]{2,1,0:T(8,128)S(1)} %get-tuple-element.5.top_in), custom_call_target="tpu_custom_call" | custom-call | tf_op jit(solution)/shard_map/pallas_call | solution.py:492

commit v6 on v5

--- a/solution.py
+++ b/solution.py
@@ -10,7 +10,7 @@
 W1, W2, HALF = 256, 512, 128
 STEPS = 8
 BUFS = 3
-CUT, REST = 296, 216
+CUT, REST = 288, 224
 CUT_PACKED, REST_PACKED = 144, 112
 NONE = 32
 PACKED = (True, True, False)
@@ -35,35 +35,35 @@
 
 
 ORDER = (
-    ("leaf", 0), ("ownx", 0, 1), ("ownz", 0), ("ownx", 0, 0), ("chains",), ("p", 0, 0), ("leaf", 2), ("ownx", 1, 1),
-    ("ownx", 1, 0), ("inv",), ("near", 0, 1), ("zpass", 0, 0), ("zpass", 0, 1), ("near", 0, 0), ("p", 0, 1),
-    ("p", 0, 2), ("p", 0, 3), ("far", 0, 1), ("far", 0, 0), ("ownz", 1), ("near", 1, 1), ("p", 0, 4), ("near", 1, 0),
-    ("ownx", 2, 1), ("ownx", 2, 0), ("p", 0, 5), ("p", 0, 6), ("p", 0, 7), ("give", 0, 0), ("zpass", 1, 0),
-    ("give", 0, 1), ("p", 1, 0), ("p", 1, 1), ("give", 0, 2), ("zpass", 1, 1), ("give", 0, 3), ("give", 0, 4),
-    ("give", 0, 5), ("far", 1, 1), ("sum", 0, 0), ("give", 0, 6), ("give", 0, 7), ("p", 1, 2), ("far", 1, 0),
-    ("sum", 0, 1), ("ownz", 2), ("near", 2, 1), ("p", 1, 3), ("near", 2, 0), ("sum", 0, 2), ("sum", 0, 3),
-    ("p", 1, 4), ("sum", 0, 4), ("ypass", 0, 1, 0), ("sum", 0, 5), ("xadd", 0, 0), ("sum", 0, 6), ("xadd", 0, 1),
-    ("sum", 0, 7), ("ypass", 0, 0, 0), ("p", 1, 5), ("ypass", 0, 1, 1), ("ypass", 0, 0, 1), ("p", 1, 6),
-    ("zpass", 2, 1), ("xadd", 0, 2), ("p", 1, 7), ("give", 1, 0), ("give", 1, 1), ("give", 1, 2), ("ylast", 0, 1),
-    ("xadd", 0, 3), ("xadd", 0, 4), ("zpass", 2, 0), ("p", 2, 0), ("xadd", 0, 5), ("give", 1, 3), ("give", 1, 4),
-    ("give", 1, 5), ("give", 1, 6), ("give", 1, 7), ("p", 2, 1), ("sum", 1, 0), ("xypass", 0, 1), ("sum", 1, 1),
-    ("xadd", 0, 6), ("sum", 1, 2), ("ylast", 0, 0), ("xadd", 0, 7), ("xypass", 0, 0), ("p", 2, 2), ("far", 2, 1),
-    ("p", 2, 3), ("finy", 0, 1), ("sum", 1, 3), ("sum", 1, 4), ("sum", 1, 5), ("sum", 1, 6), ("sum", 1, 7),
-    ("xadd", 1, 0), ("ypass", 1, 1, 0), ("ypass", 1, 0, 0), ("far", 2, 0), ("xadd", 1, 1), ("finx", 0, 1),
-    ("ypass", 1, 0, 1), ("xadd", 1, 2), ("ypass", 1, 1, 1), ("p", 2, 4), ("p", 2, 5), ("xadd", 1, 4), ("finx", 0, 0),
-    ("p", 2, 6), ("p", 2, 7), ("xypass", 1, 0), ("give", 2, 0), ("xadd", 1, 3), ("xadd", 1, 5), ("ylast", 1, 1),
-    ("finy", 0, 0), ("give", 2, 1), ("give", 2, 2), ("give", 2, 3), ("give", 2, 4), ("give", 2, 5), ("xadd", 1, 6),
-    ("give", 2, 6), ("give", 2, 7), ("ylast", 1, 0), ("xypass", 1, 1), ("give", 2, 8), ("give", 2, 9),
-    ("give", 2, 10), ("give", 2, 11), ("give", 2, 12), ("give", 2, 13), ("xadd", 1, 7), ("give", 2, 14),
-    ("give", 2, 15), ("sum", 2, 0), ("sum", 2, 1), ("sum", 2, 2), ("finy", 1, 1), ("sum", 2, 3), ("sum", 2, 4),
-    ("sum", 2, 5), ("finx", 1, 1), ("finx", 1, 0), ("finy", 1, 0), ("top", 1), ("top", 0), ("sum", 2, 6),
-    ("sum", 2, 7), ("sum", 2, 8), ("sum", 2, 9), ("xadd", 2, 0), ("sum", 2, 10), ("sum", 2, 11), ("ypass", 2, 0, 0),
-    ("ypass", 2, 1, 0), ("sum", 2, 12), ("sum", 2, 13), ("sum", 2, 14), ("xadd", 2, 1), ("sum", 2, 15),
-    ("ypass", 2, 0, 1), ("ypass", 2, 1, 1), ("xadd", 2, 2), ("xadd", 2, 3), ("xadd", 2, 4), ("xadd", 2, 5),
-    ("xypass", 2, 0), ("ylast", 2, 1), ("xadd", 2, 6), ("ylast", 2, 0), ("xypass", 2, 1), ("xadd", 2, 7),
-    ("finy", 2, 1), ("topa", 1), ("finy", 2, 0), ("topa", 0), ("finx", 2, 0), ("topb", 0), ("finx", 2, 1),
-    ("topb", 1),
+    ("leaf", 0), ("ownx", 0, 1), ("ownz", 0), ("ownx", 0, 0), ("chains",), ("ownx", 1, 1), ("p", 0, 0),
+    ("ownx", 1, 0), ("inv",), ("leaf", 2), ("zpass", 0, 0), ("zpass", 0, 1), ("near", 0, 1), ("near", 0, 0),
+    ("p", 0, 1), ("p", 0, 2), ("p", 0, 3), ("far", 0, 0), ("p", 0, 4), ("ownx", 2, 1), ("ownx", 2, 0), ("far", 0, 1),
+    ("ownz", 1), ("near", 1, 1), ("near", 1, 0), ("p", 0, 5), ("p", 0, 6), ("p", 0, 7), ("give", 0, 0),
+    ("give", 0, 1), ("give", 0, 2), ("p", 1, 0), ("zpass", 1, 0), ("zpass", 1, 1), ("give", 0, 3), ("give", 0, 4),
+    ("sum", 0, 0), ("give", 0, 5), ("give", 0, 6), ("give", 0, 7), ("sum", 0, 1), ("p", 1, 1), ("sum", 0, 2),
+    ("sum", 0, 3), ("sum", 0, 4), ("far", 1, 0), ("far", 1, 1), ("ownz", 2), ("near", 2, 0), ("near", 2, 1),
+    ("p", 1, 2), ("p", 1, 3), ("ypass", 0, 0, 0), ("xadd", 0, 0), ("ypass", 0, 1, 0), ("xadd", 0, 1), ("sum", 0, 5),
+    ("sum", 0, 6), ("sum", 0, 7), ("p", 1, 4), ("ypass", 0, 0, 1), ("ypass", 0, 1, 1), ("p", 1, 5), ("xadd", 0, 2),
+    ("p", 1, 6), ("p", 1, 7), ("give", 1, 0), ("ylast", 0, 1), ("xadd", 0, 5), ("give", 1, 1), ("zpass", 2, 1),
+    ("xadd", 0, 3), ("give", 1, 2), ("ylast", 0, 0), ("give", 1, 3), ("give", 1, 4), ("zpass", 2, 0),
+    ("xypass", 0, 1), ("xadd", 0, 4), ("give", 1, 5), ("xadd", 0, 6), ("give", 1, 6), ("give", 1, 7), ("sum", 1, 0),
+    ("xypass", 0, 0), ("p", 2, 0), ("xadd", 0, 7), ("sum", 1, 1), ("sum", 1, 2), ("sum", 1, 3), ("p", 2, 1),
+    ("p", 2, 2), ("far", 2, 0), ("finy", 0, 1), ("p", 2, 3), ("finy", 0, 0), ("ypass", 1, 0, 0), ("finx", 0, 1),
+    ("xadd", 1, 0), ("sum", 1, 4), ("sum", 1, 5), ("sum", 1, 6), ("ypass", 1, 1, 0), ("sum", 1, 7), ("far", 2, 1),
+    ("finx", 0, 0), ("xadd", 1, 1), ("ypass", 1, 0, 1), ("ypass", 1, 1, 1), ("xadd", 1, 2), ("p", 2, 4), ("p", 2, 5),
+    ("ylast", 1, 0), ("p", 2, 6), ("xadd", 1, 3), ("p", 2, 7), ("give", 2, 0), ("ylast", 1, 1), ("xadd", 1, 4),
+    ("give", 2, 1), ("xypass", 1, 0), ("xadd", 1, 5), ("xypass", 1, 1), ("xadd", 1, 6), ("give", 2, 2),
+    ("give", 2, 3), ("give", 2, 4), ("give", 2, 5), ("xadd", 1, 7), ("give", 2, 6), ("give", 2, 7), ("give", 2, 8),
+    ("sum", 2, 0), ("give", 2, 9), ("give", 2, 10), ("sum", 2, 1), ("give", 2, 11), ("give", 2, 12), ("finy", 1, 0),
+    ("give", 2, 13), ("sum", 2, 2), ("sum", 2, 3), ("give", 2, 14), ("give", 2, 15), ("sum", 2, 4), ("sum", 2, 5),
+    ("sum", 2, 6), ("finy", 1, 1), ("sum", 2, 7), ("finx", 1, 1), ("finx", 1, 0), ("sum", 2, 8), ("top", 0),
+    ("sum", 2, 9), ("sum", 2, 10), ("sum", 2, 11), ("sum", 2, 12), ("top", 1), ("sum", 2, 13), ("sum", 2, 14),
+    ("sum", 2, 15), ("ypass", 2, 0, 0), ("ypass", 2, 1, 0), ("xadd", 2, 0), ("xadd", 2, 1), ("ypass", 2, 0, 1),
+    ("ypass", 2, 1, 1), ("xadd", 2, 2), ("xadd", 2, 3), ("xadd", 2, 4), ("xadd", 2, 5), ("ylast", 2, 0),
+    ("ylast", 2, 1), ("xadd", 2, 6), ("xypass", 2, 0), ("xypass", 2, 1), ("xadd", 2, 7), ("finy", 2, 0), ("topa", 0),
+    ("finy", 2, 1), ("topa", 1), ("finx", 2, 0), ("topb", 0), ("finx", 2, 1), ("topb", 1),
 )
+
 
 def split(value):
     high = value.astype(BF16)

time: 84.5 us -> 84.3 us (level)
  no operation moved by 1% of the time
where the time goes in v6:
time: 84.3 us; the launch traced here: 84.2 us
  Pallas kernels  82.5 us (98%)
    pallas_call x1, Pallas kernels, per_device(): pl.pallas_call(kernel, out_shape=(pltpu.VMEM(leaf_rhs.shape, F32), pltpu....  81.3 us

profile of v6, /device:TPU:1, one launch (start us, length us, event | category | flops | bytes accessed | tf_op | source)
XLA Modules:
  0.0 84.2 jit_solution(8593612123283287247)
XLA Ops:
  0.6 0.7 compare_select_fusion
  1.3 0.1 copy.10
  1.4 0.1 reshape.7.wanted_in
  1.5 81.3 %shard_map.86 = (f32[1,2,256,256]{3,2,1,0:T(8,128)S(1)}, f32[2,512,256]{2,1,0:T(8,128)S(1)}) custom-call(s32[32]{0:T(128)S(1)} %reshape.7.wanted_in, f32[1,2,256,256]{3,2,1,0:T(8,128)} %leaf_rhs_in.1, f32[1,2,256,256]{3,2,1,0:T(8,128)} %leaf_inv_in.1, f32[1,2,8,2,512,256]{5,4,3,2,1,0:T(8,128)} %off_blocks.1, f32[2,512,256]{2,1,0:T(8,128)} %top_rhs.1, ...), custom_call_target="tpu_custom_call" | custom-call | flops 7500000256 | bytes 40000000 | tf_op jit(solution)/shard_map/pallas_call | solution.py:450
  82.8 1.2 %shard_map.87 = (f32[1,2,256,256]{3,2,1,0:T(8,128)}, f32[2,512,256]{2,1,0:T(8,128)}) custom-call(f32[1,2,256,256]{3,2,1,0:T(8,128)S(1)} %get-tuple-element.4.leaf_in, f32[2,512,256]{2,1,0:T(8,128)S(1)} %get-tuple-element.5.top_in), custom_call_target="tpu_custom_call" | custom-call | tf_op jit(solution)/shard_map/pallas_call | solution.py:492
